TPU v7x, 32 devices: a whole 2x2x4 slice. The times are simulated.
32 devices in a mesh: expert: 4 (over x, core), context: 2 (over y), dp: 4 (over z).
Axes of the slice: x: 2, y: 2, z: 4, core: 2. Of those that a mesh axis runs over, the one named last changes fastest.
Arguments:
- tokens: bfloat16 [16, 512, 1024], P(('expert', 'dp'), 'context'), may hold values from -6 to 6
- span_order: int32 [4], replicated, may hold values from 0 to 3, each once
- routes: int32 [16, 512, 8], P(('expert', 'dp'), 'context'), may hold values from 0 to 15, all different within a row; in each aligned block of 256 rows (0 to 255, 256 to 511, ..., all dimensions but the last counted through in order) at most 160 rows name the same one
- norm_attn: bfloat16 [1024], replicated, may hold values from 0.5 to 1.5
- w_query: bfloat16 [1024, 1024], replicated, may hold values from -0.1875 to 0.1875
- w_key: bfloat16 [1024, 512], replicated, may hold values from -0.1875 to 0.1875
- w_value: bfloat16 [1024, 512], replicated, may hold values from -0.1875 to 0.1875
- w_out: bfloat16 [1024, 1024], replicated, may hold values from -1.5 to 1.5
- norm_moe: bfloat16 [1024], replicated, may hold values from 0.5 to 1.5
- w_router: bfloat16 [1024, 16], replicated, may hold values from -0.09375 to 0.09375
- w_gate: bfloat16 [16, 1024, 512], P('expert'), may hold values from -0.1875 to 0.1875
- w_up: bfloat16 [16, 1024, 512], P('expert'), may hold values from -0.1875 to 0.1875
- w_down: bfloat16 [16, 512, 1024], P('expert'), may hold values from -1 to 1
- cotangent: bfloat16 [16, 512, 1024], P(('expert', 'dp'), 'context'), may hold values from -6 to 6
Outputs:
- outputs: bfloat16 [16, 512, 1024], P(('expert', 'dp'), 'context')
- grad_tokens: bfloat16 [16, 512, 1024], P(('expert', 'dp'), 'context')
- grad_norm_attn: float32 [1024], replicated
- grad_query: float32 [1024, 1024], replicated
- grad_key: float32 [1024, 512], replicated
- grad_value: float32 [1024, 512], replicated
- grad_out: float32 [1024, 1024], replicated
- grad_norm_moe: float32 [1024], replicated
- grad_router: float32 [1024, 16], replicated
- grad_gate: float32 [16, 1024, 512], P('expert')
- grad_up: float32 [16, 1024, 512], P('expert')
- grad_down: float32 [16, 512, 1024], P('expert')
Inputs may be any that keep to these rules, and one draw needn't show every extreme that they name: span_order is a permutation; stored block j of every sequence holds the tokens at positions span_order[j] * 128 to span_order[j] * 128 + 127. `routes`: each token names 8 different experts. Within the rows of one device (aligned blocks of 256 rows, in order), no expert is named by more than 160 rows, a bound that some block reaches.
All inputs are finite; a program needn't handle non-finite values.
Results may differ from a plain program's by a relative error of at most 0.017.
Values may be sent and summed in bfloat16 or wider, within the bound.
A program may use at most 192 MiB of HBM per device.

v0:
```python
import math

import jax
import jax.numpy as jnp
from jax import lax
from jax.sharding import PartitionSpec as P

D = 1024
H = 16
KV = 8
HD = 64
TOP = 8
EXPERTS = 16
CAP = 160
SPAN = 128


EPSILON = 1e-06
ROPE_BASE = 10000.0
MASKED = -1e30


def rope_tables(positions):
    half_dim = HD // 2
    frequency = ROPE_BASE ** (-(jnp.arange(half_dim, dtype=jnp.float32) * 2.0) / HD)
    angles = positions.astype(jnp.float32)[:, None] * frequency[None, :]
    return (jnp.cos(angles), jnp.sin(angles))


def rotate(tensor, cos_table, sin_table):
    half_dim = tensor.shape[-1] // 2
    front_half = tensor[..., :half_dim]
    back_half = tensor[..., half_dim:]
    cos_wide = cos_table[:, None, :]
    sin_wide = sin_table[:, None, :]
    return jnp.concatenate(
        [
            front_half * cos_wide - back_half * sin_wide,
            back_half * cos_wide + front_half * sin_wide,
        ],
        axis=-1,
    )


def rotate_back(tensor, cos_table, sin_table):
    half_dim = tensor.shape[-1] // 2
    front_grad = tensor[..., :half_dim]
    back_grad = tensor[..., half_dim:]
    cos_wide = cos_table[:, None, :]
    sin_wide = sin_table[:, None, :]
    return jnp.concatenate(
        [
            front_grad * cos_wide + back_grad * sin_wide,
            back_grad * cos_wide - front_grad * sin_wide,
        ],
        axis=-1,
    )


def slot_tables(route_rows):
    flat_ids = route_rows.reshape(-1)
    assignments = flat_ids.shape[0]
    one_hot = (flat_ids[:, None] == jnp.arange(EXPERTS, dtype=jnp.int32)[None, :]).astype(jnp.int32)
    earlier = jnp.cumsum(one_hot, axis=0, dtype=jnp.int32) - one_hot
    within = jnp.sum(earlier * one_hot, axis=1, dtype=jnp.int32)
    target = flat_ids * CAP + within
    source = (
        jnp.full((EXPERTS * CAP,), assignments, jnp.int32)
        .at[target]
        .set(jnp.arange(assignments, dtype=jnp.int32))
    )
    filled = source < assignments
    return (target, jnp.minimum(source, assignments - 1), filled)


def positions_of(row_index, span_order):
    block_ids = row_index // SPAN
    picked = jnp.where(
        block_ids[:, None] == jnp.arange(span_order.shape[0], dtype=jnp.int32)[None, :],
        span_order[None, :],
        0,
    )
    return jnp.sum(picked, axis=1, dtype=jnp.int32) * SPAN + row_index % SPAN


def norm_back(grad_normed, normed, inv_root):
    return inv_root * (
        grad_normed - normed * jnp.mean(grad_normed * normed, axis=-1, keepdims=True)
    )


def body(
    tokens,
    span_order,
    routes,
    norm_attn,
    w_query,
    w_key,
    w_value,
    w_out,
    norm_moe,
    w_router,
    w_gate,
    w_up,
    w_down,
    cotangent,
):
    tok_rows = tokens.shape[1]
    seq_rows = tok_rows * lax.axis_size("context")
    groups = H // KV
    score_scale = 1.0 / math.sqrt(HD)
    local_experts = w_gate.shape[0]
    expert_groups = lax.axis_size("expert")
    local_index = lax.axis_index("context") * tok_rows + jnp.arange(tok_rows, dtype=jnp.int32)
    pos_query = positions_of(local_index, span_order)
    pos_keys = positions_of(jnp.arange(seq_rows, dtype=jnp.int32), span_order)
    cos_table, sin_table = rope_tables(pos_query)
    allowed = pos_keys[None, :] <= pos_query[:, None]
    inputs = tokens[0].astype(jnp.float32)
    inv_one = lax.rsqrt(jnp.mean(inputs * inputs, axis=-1, keepdims=True) + EPSILON)
    normed_one = inputs * inv_one
    gain_one = norm_attn.astype(jnp.float32)
    h_one = (normed_one * gain_one).astype(jnp.bfloat16)
    query_pre = jnp.dot(h_one, w_query, preferred_element_type=jnp.float32).reshape(tok_rows, H, HD)
    queries = (
        rotate(query_pre, cos_table, sin_table)
        .astype(jnp.bfloat16)
        .reshape(tok_rows, KV, groups, HD)
    )
    key_pre = jnp.dot(h_one, w_key, preferred_element_type=jnp.float32).reshape(tok_rows, KV, HD)
    keys_local = (
        rotate(key_pre, cos_table, sin_table).astype(jnp.bfloat16).reshape(tok_rows, KV * HD)
    )
    values_local = jnp.dot(h_one, w_value, preferred_element_type=jnp.float32).astype(jnp.bfloat16)
    keys_all, values_all = (
        lax.all_gather(keys_local, "context", axis=0, tiled=True),
        lax.all_gather(values_local, "context", axis=0, tiled=True),
    )
    scores = (
        jnp.einsum(
            "qkgd,skd->kgqs",
            queries,
            keys_all.reshape(seq_rows, KV, HD),
            preferred_element_type=jnp.float32,
        )
        * score_scale
    )
    masked = jnp.where(allowed, scores, MASKED)
    top_score = jnp.max(masked, axis=-1, keepdims=True)
    exp_scores = jnp.exp(masked - top_score)
    total_exp = jnp.sum(exp_scores, axis=-1, keepdims=True)
    attn_probs = exp_scores / total_exp
    log_total = top_score + jnp.log(total_exp)
    mixed_heads = jnp.einsum(
        "kgqs,skd->qkgd",
        attn_probs.astype(jnp.bfloat16),
        values_all.reshape(seq_rows, KV, HD),
        preferred_element_type=jnp.float32,
    )
    mixed_heads = mixed_heads.reshape(tok_rows, H * HD).astype(jnp.bfloat16)
    y_one = inputs + jnp.dot(mixed_heads, w_out, preferred_element_type=jnp.float32)
    inv_two = lax.rsqrt(jnp.mean(y_one * y_one, axis=-1, keepdims=True) + EPSILON)
    normed_two = y_one * inv_two
    gain_two = norm_moe.astype(jnp.float32)
    h_two = (normed_two * gain_two).astype(jnp.bfloat16)
    logits = jnp.dot(h_two, w_router, preferred_element_type=jnp.float32)
    route_rows = routes[0]
    chosen_mask = route_rows[:, :, None] == jnp.arange(EXPERTS, dtype=jnp.int32)[None, None, :]
    chosen = jnp.sum(jnp.where(chosen_mask, logits[:, None, :], 0.0), axis=-1)
    chosen_exp = jnp.exp(chosen - jnp.max(chosen, axis=-1, keepdims=True))
    route_weights = chosen_exp / jnp.sum(chosen_exp, axis=-1, keepdims=True)
    target, source, filled = slot_tables(route_rows)
    sent_rows = jnp.where(
        filled[:, None], jnp.take(h_two, source // TOP, axis=0), jnp.zeros((), jnp.bfloat16)
    )
    sent_rows = sent_rows.reshape(expert_groups, local_experts, CAP, D)
    received = lax.all_to_all(sent_rows, "expert", split_axis=0, concat_axis=0, tiled=True)
    gate_pre = jnp.einsum("necd,edf->necf", received, w_gate, preferred_element_type=jnp.float32)
    upward = jnp.einsum("necd,edf->necf", received, w_up, preferred_element_type=jnp.float32)
    sigmoid_gate = jax.nn.sigmoid(gate_pre)
    silu_gate = gate_pre * sigmoid_gate
    hidden = (silu_gate * upward).astype(jnp.bfloat16)
    produced = jnp.einsum(
        "necf,efd->necd", hidden, w_down, preferred_element_type=jnp.float32
    ).astype(jnp.bfloat16)
    returned = lax.all_to_all(produced, "expert", split_axis=0, concat_axis=0, tiled=True).reshape(
        EXPERTS * CAP, D
    )
    gathered = jnp.take(returned, target, axis=0).reshape(tok_rows, TOP, D).astype(jnp.float32)
    y_two = jnp.sum(route_weights[:, :, None] * gathered, axis=1)
    outputs = (y_one + y_two).astype(jnp.bfloat16)[None]
    grad_final = cotangent[0].astype(jnp.float32)
    grad_gathered = route_weights[:, :, None] * grad_final[:, None, :]
    grad_weights = jnp.sum(grad_final[:, None, :] * gathered, axis=-1)
    grad_slots = jnp.where(
        filled[:, None], jnp.take(grad_gathered.reshape(-1, D), source, axis=0), 0.0
    )
    grad_slots = grad_slots.astype(jnp.bfloat16).reshape(expert_groups, local_experts, CAP, D)
    grad_received = lax.all_to_all(grad_slots, "expert", split_axis=0, concat_axis=0, tiled=True)
    grad_hidden = jnp.einsum(
        "necd,efd->necf", grad_received, w_down, preferred_element_type=jnp.float32
    )
    grad_down_w = jnp.einsum(
        "necf,necd->efd", hidden, grad_received, preferred_element_type=jnp.float32
    )
    grad_gate_pre = (
        grad_hidden * upward * sigmoid_gate * (1.0 + gate_pre * (1.0 - sigmoid_gate))
    ).astype(jnp.bfloat16)
    grad_up_pre = (grad_hidden * silu_gate).astype(jnp.bfloat16)
    grad_gate_w = jnp.einsum(
        "necd,necf->edf", received, grad_gate_pre, preferred_element_type=jnp.float32
    )
    grad_up_w = jnp.einsum(
        "necd,necf->edf", received, grad_up_pre, preferred_element_type=jnp.float32
    )
    grad_sent = jnp.einsum(
        "necf,edf->necd", grad_gate_pre, w_gate, preferred_element_type=jnp.float32
    )
    grad_sent = (
        grad_sent
        + jnp.einsum("necf,edf->necd", grad_up_pre, w_up, preferred_element_type=jnp.float32)
    ).astype(jnp.bfloat16)
    grad_back = lax.all_to_all(
        grad_sent, "expert", split_axis=0, concat_axis=0, tiled=True
    ).reshape(EXPERTS * CAP, D)
    grad_h_two = jnp.sum(
        jnp.take(grad_back, target, axis=0).reshape(tok_rows, TOP, D).astype(jnp.float32), axis=1
    )
    grad_chosen = route_weights * (
        grad_weights - jnp.sum(route_weights * grad_weights, axis=-1, keepdims=True)
    )
    grad_logits = jnp.sum(jnp.where(chosen_mask, grad_chosen[:, :, None], 0.0), axis=1).astype(
        jnp.bfloat16
    )
    grad_router_w = jnp.einsum("td,te->de", h_two, grad_logits, preferred_element_type=jnp.float32)
    grad_h_two = grad_h_two + jnp.einsum(
        "te,de->td", grad_logits, w_router, preferred_element_type=jnp.float32
    )
    grad_gain_two = jnp.sum(grad_h_two * normed_two, axis=0)
    grad_y_one = grad_final + norm_back(grad_h_two * gain_two, normed_two, inv_two)
    grad_attn = grad_y_one.astype(jnp.bfloat16)
    grad_out_w = jnp.einsum("tm,td->md", mixed_heads, grad_attn, preferred_element_type=jnp.float32)
    grad_mixed = jnp.einsum(
        "td,md->tm", grad_attn, w_out, preferred_element_type=jnp.float32
    ).astype(jnp.bfloat16)
    grad_mixed = grad_mixed.reshape(tok_rows, KV, groups, HD)
    keys_back, values_back = (
        lax.all_gather(keys_local, "context", axis=0, tiled=True),
        lax.all_gather(values_local, "context", axis=0, tiled=True),
    )
    key_heads = keys_back.reshape(seq_rows, KV, HD)
    scores_back = (
        jnp.einsum("qkgd,skd->kgqs", queries, key_heads, preferred_element_type=jnp.float32)
        * score_scale
    )
    probs_back = jnp.where(allowed, jnp.exp(scores_back - log_total), 0.0)
    grad_probs = jnp.einsum(
        "qkgd,skd->kgqs",
        grad_mixed,
        values_back.reshape(seq_rows, KV, HD),
        preferred_element_type=jnp.float32,
    )
    grad_values = jnp.einsum(
        "kgqs,qkgd->skd",
        probs_back.astype(jnp.bfloat16),
        grad_mixed,
        preferred_element_type=jnp.float32,
    )
    row_dots = jnp.sum(probs_back * grad_probs, axis=-1, keepdims=True)
    grad_scores = (probs_back * (grad_probs - row_dots)).astype(jnp.bfloat16)
    grad_queries = (
        jnp.einsum("kgqs,skd->qkgd", grad_scores, key_heads, preferred_element_type=jnp.float32)
        * score_scale
    )
    grad_keys = (
        jnp.einsum("kgqs,qkgd->skd", grad_scores, queries, preferred_element_type=jnp.float32)
        * score_scale
    )
    grad_keys_mine, grad_values_mine = (
        lax.psum_scatter(
            grad_keys.reshape(seq_rows, KV * HD), "context", scatter_dimension=0, tiled=True
        ),
        lax.psum_scatter(
            grad_values.reshape(seq_rows, KV * HD), "context", scatter_dimension=0, tiled=True
        ),
    )
    grad_q_pre = (
        rotate_back(grad_queries.reshape(tok_rows, H, HD), cos_table, sin_table)
        .reshape(tok_rows, H * HD)
        .astype(jnp.bfloat16)
    )
    grad_k_pre = (
        rotate_back(grad_keys_mine.reshape(tok_rows, KV, HD), cos_table, sin_table)
        .reshape(tok_rows, KV * HD)
        .astype(jnp.bfloat16)
    )
    grad_v_pre = grad_values_mine.astype(jnp.bfloat16)
    grad_query_w = jnp.einsum("td,tm->dm", h_one, grad_q_pre, preferred_element_type=jnp.float32)
    grad_key_w = jnp.einsum("td,tm->dm", h_one, grad_k_pre, preferred_element_type=jnp.float32)
    grad_value_w = jnp.einsum("td,tm->dm", h_one, grad_v_pre, preferred_element_type=jnp.float32)
    grad_h_one = jnp.einsum("tm,dm->td", grad_q_pre, w_query, preferred_element_type=jnp.float32)
    grad_h_one = grad_h_one + jnp.einsum(
        "tm,dm->td", grad_k_pre, w_key, preferred_element_type=jnp.float32
    )
    grad_h_one = grad_h_one + jnp.einsum(
        "tm,dm->td", grad_v_pre, w_value, preferred_element_type=jnp.float32
    )
    grad_gain_one = jnp.sum(grad_h_one * normed_one, axis=0)
    grad_inputs = grad_y_one + norm_back(grad_h_one * gain_one, normed_one, inv_one)
    grad_tokens = grad_inputs.astype(jnp.bfloat16)[None]
    total_gate, total_up, total_down = (
        lax.psum(grad_gate_w.astype(jnp.bfloat16), ("context", "dp")).astype(jnp.float32),
        lax.psum(grad_up_w.astype(jnp.bfloat16), ("context", "dp")).astype(jnp.float32),
        lax.psum(grad_down_w.astype(jnp.bfloat16), ("context", "dp")).astype(jnp.float32),
    )
    total_g1, total_q, total_k, total_v, total_o, total_g2, total_r = lax.psum(
        (
            grad_gain_one,
            grad_query_w,
            grad_key_w,
            grad_value_w,
            grad_out_w,
            grad_gain_two,
            grad_router_w,
        ),
        ("expert", "context", "dp"),
    )
    return (
        outputs,
        grad_tokens,
        total_g1,
        total_q,
        total_k,
        total_v,
        total_o,
        total_g2,
        total_r,
        total_gate,
        total_up,
        total_down,
    )


def solution(mesh):
    in_specs = (
        P(("expert", "dp"), "context", None),
        P(),
        P(("expert", "dp"), "context", None),
        P(),
        P(),
        P(),
        P(),
        P(),
        P(),
        P(),
        P("expert", None, None),
        P("expert", None, None),
        P("expert", None, None),
        P(("expert", "dp"), "context", None),
    )
    out_specs = (
        P(("expert", "dp"), "context", None),
        P(("expert", "dp"), "context", None),
        P(),
        P(),
        P(),
        P(),
        P(),
        P(),
        P(),
        P("expert", None, None),
        P("expert", None, None),
        P("expert", None, None),
    )
    return jax.shard_map(body, mesh=mesh, in_specs=in_specs, out_specs=out_specs, check_vma=False)
```

profile of v0, /device:TPU:0, one launch (start us, length us, event | category | flops | bytes accessed | tf_op | source)
XLA Modules:
  0.0 1157.8 jit_solution(6361689802056740667)
XLA Ops:
  13.8 9.9 all_gather.8
  30.6 8.2 all_gather.9
  53.3 4.5 reduce-window.6
  58.7 8.1 scatter_custom_fusion
  68.4 8.8 gather_fusion
  80.9 62.5 %all_to_all.20 = bf16[4,4,160,1024]{3,2,1,0:T(8,128)(2,1)S(1)} all-to-all(bf16[4,4,160,1024]{3,2,1,0:T(8,128)(2,1)S(1)} %select_select_fusion), channel_id=1, replica_groups=mesh['expert'=4,'context'=2,'dp'=4] {'expert'}, dimensions={0} | all-to-all | bytes 10485760 | tf_op jit(solution)/shard_map/all_to_all | solution.py:177
  147.4 5.4 fusion.15
  153.1 4.9 convert_bitcast_fusion.1
  161.2 5.2 all-to-all-start.1
  168.0 57.9 %all-to-all-done.1 = bf16[4,4,160,1024]{3,2,1,0:T(8,128)(2,1)} async-done(((bf16[4,4,160,1024]{3,2,1,0:T(8,128)(2,1)}), bf16[4,4,160,1024]{3,2,1,0:T(8,128)(2,1)}, u32[]{:S(2)}, u32[]{:S(2)}) %all-to-all-start.1) | async-done | bytes 5242912 | tf_op jit(solution)/shard_map/all_to_all | solution.py:186
  225.9 14.1 %gather_fusion.2 = bf16[2048,1024]{1,0:T(8,128)(2,1)} fusion(bf16[2560,1024]{1,0:T(8,128)(2,1)} %bitcast.33, s32[2048]{0:T(1024)S(1)} %broadcast_clamp_fusion), kind=kCustom, calls=%fused_computation.clone | custom fusion | bytes 8396800 | tf_op jit(solution)/shard_map/jit(_take)/gather | solution.py:189
  247.1 14.8 %gather_fusion.1 = bf16[2560,1024]{1,0:T(8,128)(2,1)} fusion(bf16[2048,1024]{1,0:T(8,128)(2,1)} %bitcast_multiply_fusion.1, s32[3072]{0:T(1024)S(1)} %pad_clamp_fusion), kind=kCustom, calls=%fused_computation.3 | custom fusion | bytes 10496000 | tf_op jit(solution)/shard_map/jit(_take)/gather | solution.py:196
  265.9 63.3 %all_to_all.21 = bf16[4,4,160,1024]{3,2,1,0:T(8,128)(2,1)} all-to-all(bf16[4,4,160,1024]{3,2,1,0:T(8,128)(2,1)S(1)} %select_convert_fusion), channel_id=1, replica_groups=mesh['expert'=4,'context'=2,'dp'=4] {'expert'}, dimensions={0} | all-to-all | bytes 10485760 | tf_op jit(solution)/shard_map/all_to_all | solution.py:199
  329.2 12.7 %fusion.13 = (bf16[4,4,160,512]{3,2,0,1:T(8,128)(2,1)}, bf16[4,4,160,512]{3,2,0,1:T(8,128)(2,1)S(1)}) fusion(f32[4,4,160,512]{3,2,1,0:T(8,128)} %get-tuple-element.56, f32[4,4,160,512]{3,2,1,0:T(8,128)} %copy-done.45, bf16[4,512,1024]{2,1,0:T(8,128)(2,1)} %param.28, bf16[4,4,160,1024]{3,2,1,0:T(8,128)(2,1)} %all_to_all.21), kind=kOutput, calls=%fused_computation.35 | convolution fusion | flops 2701393920 | bytes 25165824 | tf_op jit(solution)/shard_map/necd,efd->necf/dot_general | solution.py:200
  342.0 8.6 fusion.29
  350.6 8.9 fusion.10
  362.5 5.1 all-to-all-start.3
  367.9 59.2 %all-to-all-done.3 = bf16[4,4,160,1024]{3,2,1,0:T(8,128)(2,1)} async-done(((bf16[4,4,160,1024]{3,2,1,0:T(8,128)(2,1)}), bf16[4,4,160,1024]{3,2,1,0:T(8,128)(2,1)}, u32[]{:S(2)}, u32[]{:S(2)}) %all-to-all-start.3) | async-done | bytes 5242912 | tf_op jit(solution)/shard_map/all_to_all | solution.py:223
  427.1 14.1 %gather_fusion.3 = bf16[2048,1024]{1,0:T(8,128)(2,1)} fusion(bf16[2560,1024]{1,0:T(8,128)(2,1)} %bitcast.45, s32[2048]{0:T(1024)S(1)} %broadcast_clamp_fusion), kind=kCustom, calls=%fused_computation.1.clone | custom fusion | bytes 8396800 | tf_op jit(solution)/shard_map/jit(_take)/gather | solution.py:227
  441.2 8.1 convert_reduce_fusion
  455.5 5.3 fusion.3
  468.5 6.2 fusion.38
  475.0 8.9 bitcast_convert_fusion.2
  483.9 8.4 bitcast_convert_fusion.1
  492.4 5.1 bitcast_convert_fusion
  521.6 42.8 %all-reduce = (f32[1024]{0:T(1024)}, f32[1024]{0:T(1024)}) all-reduce(f32[1024]{0:T(1024)S(1)} %get-tuple-element.15, f32[1024]{0:T(1024)S(1)} %get-tuple-element.13), channel_id=1, replica_groups=mesh['expert'=4,'context'=2,'dp'=4] {'expert','context','dp'}, use_global_device_ids=true, to_apply=%region_24.26 | all-reduce | flops 2048 | bytes 16384 | tf_op jit(solution)/shard_map/psum | solution.py:316
  567.0 328.1 %all-reduce.8.cloned.1.call-done = (bf16[4,1024,512]{2,1,0:T(8,128)(2,1)}, bf16[4,1024,512]{2,1,0:T(8,128)(2,1)}, bf16[4,512,1024]{2,1,0:T(8,128)(2,1)}) async-done(((bf16[4,1024,512]{2,1,0:T(8,128)(2,1)}, bf16[4,1024,512]{2,1,0:T(8,128)(2,1)}, bf16[4,512,1024]{2,1,0:T(8,128)(2,1)}), (bf16[4,1024,512]{2,1,0:T(8,128)(2,1)}, bf16[4,1024,512]{2,1,0:T(8,128)(2,1)}, ...) | async-done | bytes 12582928 | tf_op jit(solution)/shard_map/psum | solution.py:312
  895.1 6.9 convert_element_type.232
  902.0 4.6 convert_element_type.234
  906.6 4.5 convert_element_type.236
  911.0 227.6 %all-reduce.6.cloned.1.call-done = (f32[1024,1024]{1,0:T(8,128)}, f32[1024,512]{1,0:T(8,128)}, f32[1024,512]{1,0:T(8,128)}, f32[1024,1024]{1,0:T(8,128)}, f32[1024,16]{0,1:T(8,128)}) async-done(((f32[1024,1024]{1,0:T(8,128)}, f32[1024,512]{1,0:T(8,128)}, f32[1024,512]{1,0:T(8,128)}, f32[1024,1024]{1,0:T(8,128)}, f32[1024,16]{0,1:T(8,128)}), (f32[1024,1024]{1,0:T(8,128)}, f32[1024,512]{1,0:T(8,128)}, ...) | async-done | bytes 12648464 | tf_op jit(solution)/shard_map/psum | solution.py:316
  1138.7 4.9 copy.142
  (210 shorter events, 103.6 us)
Async XLA Ops:
  8.0 43.3 %copy-start = (bf16[1024,1024]{1,0:T(8,128)(2,1)S(1)}, bf16[1024,1024]{1,0:T(8,128)(2,1)}, u32[]{:S(2)}) copy-start(bf16[1024,1024]{1,0:T(8,128)(2,1)} %param.23) | copy-start | bytes 6291460
  8.0 20.5 %copy-start.3 = (bf16[1,256,1024]{2,1,0:T(8,128)(2,1)S(1)}, bf16[1,256,1024]{2,1,0:T(8,128)(2,1)}, u32[]{:S(2)}) copy-start(bf16[1,256,1024]{2,1,0:T(8,128)(2,1)} %param.16) | copy-start | bytes 1572868
  10.7 32.2 %copy-start.36 = (f32[1024]{0:T(1024)}, f32[1024]{0:T(1024)S(1)}, u32[]{:S(2)}) copy-start(f32[1024]{0:T(1024)S(1)} %convert_element_type.188) | copy-start | bytes 12292
  11.9 31.0 %copy-start.41 = (f32[256]{0:T(256)}, f32[256]{0:T(256)S(1)}, u32[]{:S(2)}) copy-start(f32[256]{0:T(256)S(1)} %add_rsqrt_fusion.1) | copy-start | bytes 3076
  30.5 15.0 %copy-start.32 = (f32[256,32]{0,1:T(8,128)}, f32[256,32]{0,1:T(8,128)S(1)}, u32[]{:S(2)}) copy-start(f32[256,32]{0,1:T(8,128)S(1)} %get-tuple-element.49) | copy-start | bytes 98308
  30.5 15.0 %copy-start.34 = (f32[256,32]{0,1:T(8,128)}, f32[256,32]{0,1:T(8,128)S(1)}, u32[]{:S(2)}) copy-start(f32[256,32]{0,1:T(8,128)S(1)} %get-tuple-element.50) | copy-start | bytes 98308
  38.8 8.3 copy-start.8
  51.3 25.9 %copy-start.28 = (bf16[8,64,2,256]{3,1,2,0:T(8,128)(2,1)}, bf16[8,64,2,256]{3,1,2,0:T(8,128)(2,1)S(1)}, u32[]{:S(2)}) copy-start(bf16[8,64,2,256]{3,1,2,0:T(8,128)(2,1)S(1)} %fusion.57) | copy-start | bytes 1572868
  80.9 62.5 %copy-start.15 = (bf16[4,1024,512]{2,1,0:T(8,128)(2,1)S(1)}, bf16[4,1024,512]{2,1,0:T(8,128)(2,1)}, u32[]{:S(2)}) copy-start(bf16[4,1024,512]{2,1,0:T(8,128)(2,1)} %param.26) | copy-start | bytes 12582916
  147.4 5.6 copy-start.45
  147.4 5.6 copy-start.44
  161.2 5.3 copy-start.38
  161.2 5.5 copy-start.39
  161.2 5.7 copy-start.26
  161.2 64.7 %all-to-all-start.1 = ((bf16[4,4,160,1024]{3,2,1,0:T(8,128)(2,1)}), bf16[4,4,160,1024]{3,2,1,0:T(8,128)(2,1)}, u32[]{:S(2)}, u32[]{:S(2)}) async-start(bf16[4,4,160,1024]{3,2,1,0:T(8,128)(2,1)} %copy.89), calls=%async_computation.1 | async-start | bytes 10485760 | tf_op jit(solution)/shard_map/all_to_all | solution.py:186
  342.0 8.6 copy-start.16
  362.5 64.5 %all-to-all-start.3 = ((bf16[4,4,160,1024]{3,2,1,0:T(8,128)(2,1)}), bf16[4,4,160,1024]{3,2,1,0:T(8,128)(2,1)}, u32[]{:S(2)}, u32[]{:S(2)}) async-start(bf16[4,4,160,1024]{3,2,1,0:T(8,128)(2,1)} %copy.92), calls=%async_computation.3 | async-start | bytes 10485760 | tf_op jit(solution)/shard_map/all_to_all | solution.py:223
  367.6 140.2 %reduce-scatter.3.cloned.1.call-start = ((), (), s32[]{:S(2)}) async-start(), calls=%async_computation.6 | async-start | bytes 1572864 | tf_op jit(solution)/shard_map/reduce_scatter | solution.py:280
  441.2 8.1 copy-start.5
  441.2 8.6 copy-start.27
  449.8 5.8 copy-start.23
  455.5 5.3 slice-start
  455.5 6.1 slice-start.1
  468.4 44.2 %reduce-scatter.5.cloned.1.call-start = ((), (), s32[]{:S(2)}) async-start(), calls=%async_computation.7 | async-start | bytes 1572864 | tf_op jit(solution)/shard_map/reduce_scatter | solution.py:283
  474.7 420.3 %all-reduce.8.cloned.1.call-start = ((), (), s32[]{:S(2)}) async-start(), calls=%async_computation.9 | async-start | bytes 25165824 | tf_op jit(solution)/shard_map/psum | solution.py:312
  475.0 8.9 copy-start.17
  475.0 17.4 %slice-start.2 = ((s8[5242880]{0:T(1024)(128)(4,1)}), s8[4194304]{0:T(1024)(128)(4,1)S(1)}, s32[]{:S(2)}) async-start(s8[5242880]{0:T(1024)(128)(4,1)} %bitcast.293), calls=%async_computation.12 | async-start | bytes 8388608
  483.9 8.4 slice-start.3
  483.9 8.4 copy-start.46
  497.5 641.1 %all-reduce.6.cloned.1.call-start = ((), (), s32[]{:S(2)}) async-start(), calls=%async_computation.8 | async-start | bytes 25296896 | tf_op jit(solution)/shard_map/psum | solution.py:316
  895.1 6.9 copy-start.12
  1138.7 6.3 copy-start.24
  (25 other events, 82.1 us)
Sparse Core Ops, SparseCore 0:
  468.6 20.5 reduce-scatter.2
  492.1 20.4 reduce-scatter.4
Sparse Core Ops, SparseCore 1:
  497.6 397.4 all-reduce.7
  903.6 235.0 all-reduce.5
where the time goes:
time: 1170 us; the launch traced here: 1160 us
  waiting for transfers between devices  675 us (58%)
  blocking collectives  187 us (16%)
  matrix products  114 us (10%)
  local copies, waits for them, and re-layouts  94.5 us (8%)
  other arithmetic  60.2 us (5%)
  between operations  16.8 us (1%)
    psum x1, waiting for transfers between devices, body(): lax.psum(grad_gate_w.astype(jnp.bfloat16), ('context', 'dp'))  328 us
    psum x1, waiting for transfers between devices, body(): lax.psum((grad_gain_one, grad_query_w, grad_key_w, grad_value_w, grad_out...  228 us
    all_to_all x1, blocking collectives, body(): lax.all_to_all(grad_slots, 'expert', split_axis=0, concat_axis=0, tiled=T...  63.3 us
    all_to_all x1, blocking collectives, body(): lax.all_to_all(sent_rows, 'expert', split_axis=0, concat_axis=0, tiled=True)  62.5 us
    all_to_all x1, waiting for transfers between devices, body(): lax.all_to_all(grad_sent, 'expert', split_axis=0, concat_axis=0, tiled=True)  59.2 us
    all_to_all x1, waiting for transfers between devices, body(): lax.all_to_all(produced, 'expert', split_axis=0, concat_axis=0, tiled=True)  57.9 us
    psum x1, blocking collectives, body(): lax.psum((grad_gain_one, grad_query_w, grad_key_w, grad_value_w, grad_out...  42.8 us
    unnamed x110, local copies, waits for them, and re-layouts  23.9 us
  transfers between devices with their start and end apart: 6, of which 5 were waited for; matrix products, arithmetic and copies ran while one was open for 6% of the time, Pallas kernels for 0%

commit v1 on v0

v1 whole, which is shorter than its diff:
```python
import math

import jax
import jax.numpy as jnp
from jax import lax
from jax.sharding import PartitionSpec as P

H = 16
KV = 8
HD = 64
EXPERTS = 16
SPAN = 128

EPSILON = 1e-06
ROPE_BASE = 10000.0
MASKED = -1e30
F32 = jnp.float32
BF16 = jnp.bfloat16


def rope_tables(positions):
    half_dim = HD // 2
    frequency = ROPE_BASE ** (-(jnp.arange(half_dim, dtype=F32) * 2.0) / HD)
    angles = positions.astype(F32)[:, None] * frequency[None, :]
    return (jnp.cos(angles), jnp.sin(angles))


def rotate(tensor, cos_table, sin_table):
    half_dim = tensor.shape[-1] // 2
    front = tensor[..., :half_dim]
    back = tensor[..., half_dim:]
    cos_wide = cos_table[:, None, :]
    sin_wide = sin_table[:, None, :]
    return jnp.concatenate(
        [front * cos_wide - back * sin_wide, back * cos_wide + front * sin_wide], axis=-1
    )


def positions_of(row_index, span_order):
    block_ids = row_index // SPAN
    picked = jnp.where(
        block_ids[:, None] == jnp.arange(span_order.shape[0], dtype=jnp.int32)[None, :],
        span_order[None, :],
        0,
    )
    return jnp.sum(picked, axis=1, dtype=jnp.int32) * SPAN + row_index % SPAN


def norm_back(grad_normed, normed, inv_root):
    return inv_root * (
        grad_normed - normed * jnp.mean(grad_normed * normed, axis=-1, keepdims=True)
    )


def dot(a, b):
    return jnp.dot(a, b, preferred_element_type=F32)


def dot_t(a, b):
    return lax.dot_general(a, b, (((1,), (1,)), ((), ())), preferred_element_type=F32)


def t_dot(a, b):
    return lax.dot_general(a, b, (((0,), (0,)), ((), ())), preferred_element_type=F32)


def body(
    tokens,
    span_order,
    routes,
    norm_attn,
    w_query,
    w_key,
    w_value,
    w_out,
    norm_moe,
    w_router,
    w_gate,
    w_up,
    w_down,
    cotangent,
):
    tok_rows = tokens.shape[1]
    width = tokens.shape[2]
    seq_rows = tok_rows * lax.axis_size("context")
    groups = H // KV
    score_scale = 1.0 / math.sqrt(HD)
    local_experts = w_gate.shape[0]
    ff = w_gate.shape[2]
    dy_all = lax.all_gather(cotangent[0], "expert", axis=0, tiled=True)
    routes_all = lax.all_gather(routes[0], "expert", axis=0, tiled=True)

    local_index = lax.axis_index("context") * tok_rows + jnp.arange(tok_rows, dtype=jnp.int32)
    pos_query = positions_of(local_index, span_order)
    pos_keys = positions_of(jnp.arange(seq_rows, dtype=jnp.int32), span_order)
    cos_table, sin_table = rope_tables(pos_query)
    allowed = pos_keys[None, :] <= pos_query[:, None]
    inputs = tokens[0].astype(F32)
    inv_one = lax.rsqrt(jnp.mean(inputs * inputs, axis=-1, keepdims=True) + EPSILON)
    normed_one = inputs * inv_one
    gain_one = norm_attn.astype(F32)
    h_one = (normed_one * gain_one).astype(BF16)
    key_pre = dot(h_one, w_key).reshape(tok_rows, KV, HD)
    keys_local = rotate(key_pre, cos_table, sin_table).astype(BF16).reshape(tok_rows, KV * HD)
    values_local = dot(h_one, w_value).astype(BF16)
    kv_all = lax.all_gather(
        jnp.concatenate([keys_local, values_local], axis=1), "context", axis=0, tiled=True
    )
    query_pre = dot(h_one, w_query).reshape(tok_rows, H, HD)
    queries = (
        rotate(query_pre, cos_table, sin_table).astype(BF16).reshape(tok_rows, KV, groups, HD)
    )
    keys_all = kv_all[:, : KV * HD].reshape(seq_rows, KV, HD)
    values_all = kv_all[:, KV * HD :].reshape(seq_rows, KV, HD)
    scores = (
        jnp.einsum("qkgd,skd->kgqs", queries, keys_all, preferred_element_type=F32) * score_scale
    )
    masked = jnp.where(allowed, scores, MASKED)
    top_score = jnp.max(masked, axis=-1, keepdims=True)
    exp_scores = jnp.exp(masked - top_score)
    total_exp = jnp.sum(exp_scores, axis=-1, keepdims=True)
    attn_probs = exp_scores / total_exp
    probs_rounded = attn_probs.astype(BF16)
    mixed_heads = jnp.einsum(
        "kgqs,skd->qkgd", probs_rounded, values_all, preferred_element_type=F32
    )
    mixed_heads = mixed_heads.reshape(tok_rows, H * HD).astype(BF16)
    y_one = inputs + dot(mixed_heads, w_out)
    inv_two = lax.rsqrt(jnp.mean(y_one * y_one, axis=-1, keepdims=True) + EPSILON)
    normed_two = y_one * inv_two
    gain_two = norm_moe.astype(F32)
    h_two = (normed_two * gain_two).astype(BF16)
    h_all = lax.all_gather(h_two, "expert", axis=0, tiled=True)

    experts = jnp.arange(EXPERTS, dtype=jnp.int32)
    chosen = jnp.any(routes_all[:, :, None] == experts[None, None, :], axis=1)
    logits = jnp.where(chosen, dot(h_all, w_router), MASKED)
    weights = jnp.where(chosen, jnp.exp(logits - jnp.max(logits, axis=-1, keepdims=True)), 0.0)
    weights = weights / jnp.sum(weights, axis=-1, keepdims=True)
    me = lax.axis_index("expert")
    mine = lax.dynamic_slice_in_dim(weights, me * local_experts, local_experts, axis=1)

    partial_y = None
    partial_h = None
    dots = []
    g_gate, g_up, g_down = [], [], []
    for e in range(local_experts):
        weight = mine[:, e : e + 1]
        gate_pre = dot(h_all, w_gate[e])
        upward = dot(h_all, w_up[e])
        back = dot_t(dy_all, w_down[e])
        sigmoid_gate = jax.nn.sigmoid(gate_pre)
        silu_gate = gate_pre * sigmoid_gate
        hidden = silu_gate * upward
        hidden_w = (hidden * weight).astype(BF16)
        dots.append(jnp.sum(hidden * back, axis=-1, keepdims=True))
        grad_hidden = back * weight
        grad_gate_pre = (
            grad_hidden * upward * sigmoid_gate * (1.0 + gate_pre * (1.0 - sigmoid_gate))
        ).astype(BF16)
        grad_up_pre = (grad_hidden * silu_gate).astype(BF16)
        add_y = dot(hidden_w, w_down[e])
        add_h = dot_t(grad_gate_pre, w_gate[e]) + dot_t(grad_up_pre, w_up[e])
        partial_y = add_y if partial_y is None else partial_y + add_y
        partial_h = add_h if partial_h is None else partial_h + add_h
        g_down.append(t_dot(hidden_w, dy_all).astype(BF16))
        g_gate.append(t_dot(h_all, grad_gate_pre).astype(BF16))
        g_up.append(t_dot(h_all, grad_up_pre).astype(BF16))

    d_weights = jnp.concatenate(dots, axis=1)
    d_wide = lax.dynamic_update_slice_in_dim(
        jnp.zeros((d_weights.shape[0], EXPERTS), F32), d_weights, me * local_experts, axis=1
    )
    d_high = lax.reduce_precision(d_wide, 8, 7)
    packed = jnp.concatenate(
        [
            partial_h.astype(BF16),
            d_high.astype(BF16),
            (d_wide - d_high).astype(BF16),
            jnp.zeros((d_wide.shape[0], 128 - 2 * EXPERTS), BF16),
        ],
        axis=1,
    )
    home = lax.psum_scatter(packed, "expert", scatter_dimension=0, tiled=True).astype(F32)
    y_two = lax.psum_scatter(
        partial_y.astype(BF16), "expert", scatter_dimension=0, tiled=True
    ).astype(F32)
    total_gate, total_up, total_down = (
        lax.psum(jnp.stack(g), ("context", "dp")).astype(F32) for g in (g_gate, g_up, g_down)
    )
    outputs = (y_one + y_two).astype(BF16)[None]

    grad_final = cotangent[0].astype(F32)
    grad_weights = home[:, width : width + EXPERTS] + home[:, width + EXPERTS : width + 2 * EXPERTS]
    own = lax.dynamic_slice_in_dim(weights, me * tok_rows, tok_rows, axis=0)
    grad_logits = (
        own * (grad_weights - jnp.sum(own * grad_weights, axis=-1, keepdims=True))
    ).astype(BF16)
    grad_router_w = t_dot(h_two, grad_logits)
    grad_h_two = home[:, :width] + dot_t(grad_logits, w_router)
    grad_gain_two = jnp.sum(grad_h_two * normed_two, axis=0)
    grad_y_one = grad_final + norm_back(grad_h_two * gain_two, normed_two, inv_two)
    grad_attn = grad_y_one.astype(BF16)
    grad_out_w = t_dot(mixed_heads, grad_attn)
    grad_mixed = dot_t(grad_attn, w_out).astype(BF16).reshape(tok_rows, KV, groups, HD)
    grad_probs = jnp.einsum("qkgd,skd->kgqs", grad_mixed, values_all, preferred_element_type=F32)
    grad_values = jnp.einsum(
        "kgqs,qkgd->skd", probs_rounded, grad_mixed, preferred_element_type=F32
    )
    row_dots = jnp.sum(attn_probs * grad_probs, axis=-1, keepdims=True)
    grad_scores = (attn_probs * (grad_probs - row_dots)).astype(BF16)
    grad_keys = (
        jnp.einsum("kgqs,qkgd->skd", grad_scores, queries, preferred_element_type=F32)
        * score_scale
    )
    grad_kv = lax.psum_scatter(
        jnp.concatenate(
            [grad_keys.reshape(seq_rows, KV * HD), grad_values.reshape(seq_rows, KV * HD)], axis=1
        ).astype(BF16),
        "context",
        scatter_dimension=0,
        tiled=True,
    ).astype(F32)
    grad_queries = (
        jnp.einsum("kgqs,skd->qkgd", grad_scores, keys_all, preferred_element_type=F32)
        * score_scale
    )
    grad_q_pre = (
        rotate(grad_queries.reshape(tok_rows, H, HD), cos_table, -sin_table)
        .reshape(tok_rows, H * HD)
        .astype(BF16)
    )
    grad_k_pre = (
        rotate(grad_kv[:, : KV * HD].reshape(tok_rows, KV, HD), cos_table, -sin_table)
        .reshape(tok_rows, KV * HD)
        .astype(BF16)
    )
    grad_v_pre = grad_kv[:, KV * HD :].astype(BF16)
    grad_query_w = t_dot(h_one, grad_q_pre)
    grad_key_w = t_dot(h_one, grad_k_pre)
    grad_value_w = t_dot(h_one, grad_v_pre)
    grad_h_one = (
        dot_t(grad_q_pre, w_query) + dot_t(grad_k_pre, w_key) + dot_t(grad_v_pre, w_value)
    )
    grad_gain_one = jnp.sum(grad_h_one * normed_one, axis=0)
    grad_inputs = grad_y_one + norm_back(grad_h_one * gain_one, normed_one, inv_one)
    grad_tokens = grad_inputs.astype(BF16)[None]
    everywhere = ("expert", "context", "dp")
    total_o = lax.psum(grad_out_w.astype(BF16), everywhere).astype(F32)
    total_q, total_k, total_v = (
        t.astype(F32)
        for t in lax.psum(
            tuple(g.astype(BF16) for g in (grad_query_w, grad_key_w, grad_value_w)), everywhere
        )
    )
    total_g1, total_g2, total_r = lax.psum(
        (grad_gain_one, grad_gain_two, grad_router_w), everywhere
    )
    return (
        outputs,
        grad_tokens,
        total_g1,
        total_q,
        total_k,
        total_v,
        total_o,
        total_g2,
        total_r,
        total_gate,
        total_up,
        total_down,
    )


def solution(mesh):
    in_specs = (
        P(("expert", "dp"), "context", None),
        P(),
        P(("expert", "dp"), "context", None),
        P(),
        P(),
        P(),
        P(),
        P(),
        P(),
        P(),
        P("expert", None, None),
        P("expert", None, None),
        P("expert", None, None),
        P(("expert", "dp"), "context", None),
    )
    out_specs = (
        P(("expert", "dp"), "context", None),
        P(("expert", "dp"), "context", None),
        P(),
        P(),
        P(),
        P(),
        P(),
        P(),
        P(),
        P("expert", None, None),
        P("expert", None, None),
        P("expert", None, None),
    )
    return jax.shard_map(body, mesh=mesh, in_specs=in_specs, out_specs=out_specs, check_vma=False)
```

time: 1170 us -> 968 us (0.83)
  blocking collectives: 187 us -> 45.5 us
  local copies, waits for them, and re-layouts: 94.5 us -> 32.3 us
  matrix products: 114 us -> 145 us
    all_to_all x2 -> x0, blocking collectives: 126 us -> none  [the longest x1 63.3 us: body(): lax.all_to_all(grad_slots, 'expert', split_axis=0, concat_axis=0, tiled=T...]
    all_to_all x2 -> x0, waiting for transfers between devices: 117 us -> none  [the longest x1 59.2 us: body(): lax.all_to_all(grad_sent, 'expert', split_axis=0, concat_axis=0, tiled=True)]
    gather x4 -> x0, local copies, waits for them, and re-layouts: 51.8 us -> none  [the longest x1 14.8 us: body(): jnp.take(grad_gathered.reshape(-1, D), source, axis=0)]
    reduce_scatter x2 -> x3, waiting for transfers between devices: 1.83 us -> 49.2 us  [the longest x1 30.9 us: body(): lax.psum_scatter(partial_y.astype(BF16), 'expert', scatter_dimension=0, t...]
    psum x2 -> x3, waiting for transfers between devices: 556 us -> 592 us  [the longest x1 394 us: body(): lax.psum(jnp.stack(g), ('context', 'dp')).astype(F32)]
    all_gather x0 -> x3, waiting for transfers between devices: none -> 26.8 us  [the longest x1 15.2 us: body(): lax.all_gather(jnp.concatenate([keys_local, values_local], axis=1), 'cont...]
    dot_general x29 -> x55, matrix products: 112 us -> 135 us  [the longest x17 47.3 us: dot_t(): lax.dot_general(a, b, (((1,), (1,)), ((), ())), preferred_element_type=F32)]
    reduce_sum x8 -> x2, other arithmetic: 13.3 us -> 0.06 us  [the longest x1 0.03 us: body(): weights = weights / jnp.sum(weights, axis=-1, keepdims=True)]
  transfers between devices with their start and end apart: 6 -> 9, of which waited for: 5 -> 8; matrix products, arithmetic and copies ran while one was open for 6% -> 13% of each run, Pallas kernels for 0% -> 0%
where the time goes in v1:
time: 968 us; the launch traced here: 959 us
  waiting for transfers between devices  668 us (69%)
  matrix products  145 us (15%)
  other arithmetic  52.2 us (5%)
  blocking collectives  45.5 us (5%)
  local copies, waits for them, and re-layouts  32.3 us (3%)
  between operations  15.3 us (2%)
    psum x1, waiting for transfers between devices, body(): lax.psum(jnp.stack(g), ('context', 'dp')).astype(F32)  394 us
    psum x1, waiting for transfers between devices, body(): lax.psum((grad_gain_one, grad_gain_two, grad_router_w), everywhere)  108 us
    psum x1, waiting for transfers between devices, body(): lax.psum(tuple((g.astype(BF16) for g in (grad_query_w, grad_key_w, grad_v...  89.7 us
    dot_general x17, matrix products, dot_t(): lax.dot_general(a, b, (((1,), (1,)), ((), ())), preferred_element_type=F32)  47.3 us
    psum x1, blocking collectives, body(): lax.psum((grad_gain_one, grad_gain_two, grad_router_w), everywhere)  40.1 us
    dot_general x17, matrix products, dot(): return jnp.dot(a, b, preferred_element_type=F32)  37.4 us
    dot_general x17, matrix products, t_dot(): lax.dot_general(a, b, (((0,), (0,)), ((), ())), preferred_element_type=F32)  35.9 us
    reduce_scatter x1, waiting for transfers between devices, body(): lax.psum_scatter(partial_y.astype(BF16), 'expert', scatter_dimension=0, t...  30.9 us
  transfers between devices with their start and end apart: 9, of which 8 were waited for; matrix products, arithmetic and copies ran while one was open for 13% of the time, Pallas kernels for 0%

profile of v1, /device:TPU:0, one launch (start us, length us, event | category | flops | bytes accessed | tf_op | source)
XLA Modules:
  0.0 959.3 jit_solution(15199929937461508150)
XLA Ops:
  19.1 3.9 copy.122
  27.2 15.2 %all-gather.6.cloned.1.call-done = bf16[512,1024]{1,0:T(8,128)(2,1)} async-done(((bf16[256,1024]{1,0:T(8,128)(2,1)}), bf16[512,1024]{1,0:T(8,128)(2,1)}) %all-gather.6.cloned.1.call-update) | async-done | bytes 1048592 | tf_op jit(solution)/shard_map/all_gather | solution.py:106
  46.7 8.0 fusion.203
  54.7 4.3 fusion.74
  62.2 5.4 all-gather
  67.7 4.6 fusion.16
  80.1 11.5 %all-gather.8.cloned.1.call-done = bf16[1024,1024]{0,1:T(8,128)(2,1)} async-done(((bf16[256,1024]{0,1:T(8,128)(2,1)}), bf16[1024,1024]{0,1:T(8,128)(2,1)}) %all-gather.8.cloned.1.call-update) | async-done | bytes 2097168 | tf_op jit(solution)/shard_map/all_gather | solution.py:133
  102.8 3.8 multiply_convert_fusion.1
  109.3 3.5 multiply_convert_fusion.5
  112.8 3.5 multiply_convert_fusion.7
  127.5 3.7 fusion.129
  131.2 3.3 fusion.125
  134.5 9.2 add_convert_fusion
  157.3 4.3 fusion.47
  168.4 11.4 %reduce-scatter.6.cloned.1.call-done = bf16[256,1152]{0,1:T(8,128)(2,1)} async-done(((bf16[1024,1152]{0,1:T(8,128)(2,1)}), bf16[256,1152]{0,1:T(8,128)(2,1)}) %reduce-scatter.6.cloned.1.call-update) | async-done | bytes 589840 | tf_op jit(solution)/shard_map/reduce_scatter | solution.py:184
  183.4 30.9 %reduce-scatter.4.cloned.1.call-done = bf16[256,1024]{0,1:T(8,128)(2,1)} async-done(((bf16[1024,1024]{0,1:T(8,128)(2,1)}), bf16[256,1024]{0,1:T(8,128)(2,1)}) %reduce-scatter.4.cloned.1.call-update) | async-done | bytes 524304 | tf_op jit(solution)/shard_map/reduce_scatter | solution.py:185
  219.8 4.9 fusion.1
  224.8 4.8 fusion.78
  229.6 4.5 fusion.3
  237.7 4.0 fusion.51
  250.8 6.9 reduce-scatter.8.cloned.1.call-done
  261.9 3.3 fusion.49
  276.7 3.8 pad_maximum_fusion
  284.3 3.4 fusion.206
  292.4 40.1 %all-reduce = (f32[1024]{0:T(1024)}, f32[1024]{0:T(1024)}) all-reduce(f32[1024]{0:T(1024)S(1)} %get-tuple-element.26, f32[1024]{0:T(1024)S(1)} %get-tuple-element.24), channel_id=1, replica_groups=mesh['expert'=4,'context'=2,'dp'=4] {'expert','context','dp'}, use_global_device_ids=true, to_apply=%region_21.22 | all-reduce | flops 2048 | bytes 16384 | tf_op jit(solution)/shard_map/psum | solution.py:256
  332.6 89.7 %all-reduce.9.cloned.1.call-done = (bf16[1024,1024]{1,0:T(8,128)(2,1)}, bf16[1024,512]{1,0:T(8,128)(2,1)}, bf16[1024,512]{1,0:T(8,128)(2,1)}, bf16[1024,1024]{1,0:T(8,128)(2,1)}) async-done(((bf16[1024,1024]{1,0:T(8,128)(2,1)}, bf16[1024,512]{1,0:T(8,128)(2,1)}, bf16[1024,512]{1,0:T(8,128)(2,1)}, bf16[1024,1024]{1,0:T(8,128)(2,1)}), (bf16[1024,1024]{1,0:T(8,128)(2,1)}, bf16[1024,512]{1,0:T(8,128)(2,1)}, ...) | async-done | bytes 6291472 | tf_op jit(solution)/shard_map/psum | solution.py:252
  422.2 4.2 convert_element_type.280
  432.8 394.3 %all-reduce.11.cloned.1.call-done = (bf16[4,1024,512]{2,1,0:T(8,128)(2,1)}, bf16[4,1024,512]{2,1,0:T(8,128)(2,1)}, bf16[4,512,1024]{2,1,0:T(8,128)(2,1)}) async-done(((bf16[4,1024,512]{2,1,0:T(8,128)(2,1)}, bf16[4,1024,512]{2,1,0:T(8,128)(2,1)}, bf16[4,512,1024]{2,1,0:T(8,128)(2,1)}), (bf16[4,1024,512]{2,1,0:T(8,128)(2,1)}, bf16[4,1024,512]{2,1,0:T(8,128)(2,1)}, ...) | async-done | bytes 12582928 | tf_op jit(solution)/shard_map/psum | solution.py:189
  827.2 6.9 convert_element_type.291
  834.1 4.6 convert_element_type.296
  838.7 4.4 convert_element_type.301
  843.1 107.7 %all-reduce.7.cloned.1.call-done = f32[1024,16]{0,1:T(8,128)} async-done(((f32[1024,16]{0,1:T(8,128)}), f32[1024,16]{0,1:T(8,128)}) %all-reduce.7.cloned.1.call-update) | async-done | bytes 65552 | tf_op jit(solution)/shard_map/psum | solution.py:256
  (296 shorter events, 129.9 us)
Async XLA Ops:
  7.2 51.9 %copy-start = (bf16[1024,1024]{1,0:T(8,128)(2,1)S(1)}, bf16[1024,1024]{1,0:T(8,128)(2,1)}, u32[]{:S(2)}) copy-start(bf16[1024,1024]{1,0:T(8,128)(2,1)} %param.21) | copy-start | bytes 6291460
  7.2 35.2 %all-gather.6.cloned.1.call-start = ((), (), s32[]{:S(2)}) async-start(), calls=%async_computation.3 | async-start | bytes 1572864 | tf_op jit(solution)/shard_map/all_gather | solution.py:106
  8.6 50.4 %copy-start.3 = (bf16[1,256,1024]{1,2,0:T(8,128)(2,1)}, bf16[1,256,1024]{1,2,0:T(8,128)(2,1)S(1)}, u32[]{:S(2)}) copy-start(bf16[1,256,1024]{1,2,0:T(8,128)(2,1)S(1)} %copy.116) | copy-start | bytes 1572868
  9.4 13.6 %copy-start.62 = (f32[1024]{0:T(1024)}, f32[1024]{0:T(1024)S(1)}, u32[]{:S(2)}) copy-start(f32[1024]{0:T(1024)S(1)} %convert_element_type.237) | copy-start | bytes 12292
  9.5 13.5 %copy-start.64 = (f32[256]{0:T(256)}, f32[256]{0:T(256)S(1)}, u32[]{:S(2)}) copy-start(f32[256]{0:T(256)S(1)} %add_rsqrt_fusion.1) | copy-start | bytes 3076
  16.1 10.2 %copy-start.47 = (f32[256,32]{0,1:T(8,128)}, f32[256,32]{0,1:T(8,128)S(1)}, u32[]{:S(2)}) copy-start(f32[256,32]{0,1:T(8,128)S(1)} %get-tuple-element.75) | copy-start | bytes 98308
  18.2 49.5 %all-gather.10.cloned.1.call-start = ((), (), s32[]{:S(2)}) async-start(), calls=%async_computation.9 | async-start | bytes 2621440 | tf_op jit(solution)/shard_map/all_gather | solution.py:90
  18.9 72.7 %all-gather.8.cloned.1.call-start = ((), (), s32[]{:S(2)}) async-start(), calls=%async_computation.4 | async-start | bytes 2621440 | tf_op jit(solution)/shard_map/all_gather | solution.py:133
  27.2 19.6 %copy-start.43 = (bf16[256,16,32]{0,2,1:T(8,128)(2,1)}, bf16[256,16,32]{0,2,1:T(8,128)(2,1)S(1)}, u32[]{:S(2)}) copy-start(bf16[256,16,32]{0,2,1:T(8,128)(2,1)S(1)} %get-tuple-element.57) | copy-start | bytes 786436
  27.2 19.6 %copy-start.61 = (pred[256,512]{0,1:T(8,128)(4,1)S(1)}, pred[256,512]{0,1:T(8,128)(4,1)}, u32[]{:S(2)}) copy-start(pred[256,512]{0,1:T(8,128)(4,1)} %broadcast_compare_fusion) | copy-start | bytes 393220
  46.7 8.0 copy-start.15
  62.1 117.7 %reduce-scatter.6.cloned.1.call-start = ((), (), s32[]{:S(2)}) async-start(), calls=%async_computation.6 | async-start | bytes 2949120 | tf_op jit(solution)/shard_map/reduce_scatter | solution.py:184
  67.7 4.6 copy-start.13
  77.5 14.1 %copy-start.59 = (bf16[1024,16]{0,1:T(8,128)(2,1)S(1)}, bf16[1024,16]{0,1:T(8,128)(2,1)}, u32[]{:S(2)}) copy-start(bf16[1024,16]{0,1:T(8,128)(2,1)} %param.23) | copy-start | bytes 98308
  106.6 10.6 %copy-start.78 = (bf16[1024,512]{0,1:T(8,128)(2,1)}, bf16[1024,512]{0,1:T(8,128)(2,1)S(1)}, u32[]{:S(2)}) copy-start(bf16[1024,512]{0,1:T(8,128)(2,1)S(1)} %get-tuple-element.45) | copy-start | bytes 3145732
  109.3 9.1 copy-start.79
  109.3 10.4 %copy-start.76 = (bf16[1024,512]{0,1:T(8,128)(2,1)}, bf16[1024,512]{0,1:T(8,128)(2,1)S(1)}, u32[]{:S(2)}) copy-start(bf16[1024,512]{0,1:T(8,128)(2,1)S(1)} %get-tuple-element.53) | copy-start | bytes 3145732
  109.3 37.3 %copy-start.24 = (bf16[1024,512]{0,1:T(8,128)(2,1)}, bf16[1024,512]{0,1:T(8,128)(2,1)S(1)}, u32[]{:S(2)}) copy-start(bf16[1024,512]{0,1:T(8,128)(2,1)S(1)} %get-tuple-element.54) | copy-start | bytes 3145732
  112.8 8.1 copy-start.81
  112.8 11.4 %copy-start.73 = (bf16[1024,512]{0,1:T(8,128)(2,1)}, bf16[1024,512]{0,1:T(8,128)(2,1)S(1)}, u32[]{:S(2)}) copy-start(bf16[1024,512]{0,1:T(8,128)(2,1)S(1)} %get-tuple-element.51) | copy-start | bytes 3145732
  116.4 11.2 %copy-start.83 = (bf16[1024,512]{0,1:T(8,128)(2,1)}, bf16[1024,512]{0,1:T(8,128)(2,1)S(1)}, u32[]{:S(2)}) copy-start(bf16[1024,512]{0,1:T(8,128)(2,1)S(1)} %get-tuple-element.39) | copy-start | bytes 3145732
  116.4 14.8 %copy-start.74 = (bf16[1024,512]{0,1:T(8,128)(2,1)}, bf16[1024,512]{0,1:T(8,128)(2,1)S(1)}, u32[]{:S(2)}) copy-start(bf16[1024,512]{0,1:T(8,128)(2,1)S(1)} %get-tuple-element.49) | copy-start | bytes 3145732
  146.6 67.8 %reduce-scatter.4.cloned.1.call-start = ((), (), s32[]{:S(2)}) async-start(), calls=%async_computation.5 | async-start | bytes 2621440 | tf_op jit(solution)/shard_map/reduce_scatter | solution.py:185
  155.2 102.5 %reduce-scatter.8.cloned.1.call-start = ((), (), s32[]{:S(2)}) async-start(), calls=%async_computation.7 | async-start | bytes 1572864 | tf_op jit(solution)/shard_map/reduce_scatter | solution.py:216
  166.1 14.8 %copy-start.58 = (f32[1024,16]{0,1:T(8,128)S(1)}, f32[1024,16]{0,1:T(8,128)}, u32[]{:S(2)}) copy-start(f32[1024,16]{0,1:T(8,128)} %copy-done.57) | copy-start | bytes 196612
  166.1 15.8 %copy-start.9 = (f32[256,1024]{0,1:T(8,128)S(1)}, f32[256,1024]{0,1:T(8,128)}, u32[]{:S(2)}) copy-start(f32[256,1024]{0,1:T(8,128)} %copy-done.8) | copy-start | bytes 3145732
  166.1 15.8 %copy-start.60 = (bf16[1024,16]{0,1:T(8,128)(2,1)S(1)}, bf16[1024,16]{0,1:T(8,128)(2,1)}, u32[]{:S(2)}) copy-start(bf16[1024,16]{0,1:T(8,128)(2,1)} %param.23) | copy-start | bytes 98308
  219.8 4.9 copy-start.54
  237.2 185.0 %all-reduce.9.cloned.1.call-start = ((), (), s32[]{:S(2)}) async-start(), calls=%async_computation.10 | async-start | bytes 12582912 | tf_op jit(solution)/shard_map/psum | solution.py:252
  261.8 565.4 %all-reduce.11.cloned.1.call-start = ((), (), s32[]{:S(2)}) async-start(), calls=%async_computation.11 | async-start | bytes 25165824 | tf_op jit(solution)/shard_map/psum | solution.py:189
  280.5 670.3 %all-reduce.7.cloned.1.call-start = ((), (), s32[]{:S(2)}) async-start(), calls=%async_computation.8 | async-start | bytes 131072 | tf_op jit(solution)/shard_map/psum | solution.py:256
  827.2 6.9 copy-start.12
  (66 other events, 161.2 us)
Sparse Core Ops, SparseCore 0:
  18.3 24.0 all-gather.5
  43.9 22.5 all-gather.9
  68.7 22.9 all-gather.7
  146.7 33.0 reduce-scatter.5
  182.9 31.4 reduce-scatter.3
  237.3 20.3 reduce-scatter.7
  265.3 156.8 all-reduce.8
  427.5 399.6 all-reduce.10
  834.2 116.5 all-reduce.6

commit v2 on v1

--- a/solution.py
+++ b/solution.py
@@ -62,6 +62,49 @@
 
 def t_dot(a, b):
     return lax.dot_general(a, b, (((0,), (0,)), ((), ())), preferred_element_type=F32)
+
+
+def ring_sum(gate, up, down):
+    axes = ("context", "dp")
+    inner = lax.axis_size("dp")
+    size = lax.axis_size("context") * inner
+    place = [
+        c * inner + (d if c % 2 == 0 else inner - 1 - d)
+        for c in range(size // inner)
+        for d in range(inner)
+    ]
+    order = sorted(range(size), key=lambda i: place[i])
+    pos = jnp.array(place, jnp.int32)[lax.axis_index(axes)]
+    shapes = [a.shape for a in (gate, up, down)]
+    gate, up, down = (a.reshape(2, size, -1, a.shape[-1]) for a in (gate, up, down))
+    rows, half = gate.shape[2], gate.shape[3]
+
+    def piece(way, index):
+        g, u, d = (
+            lax.dynamic_index_in_dim(a[way], index, 0, keepdims=False) for a in (gate, up, down)
+        )
+        return jnp.concatenate([jnp.concatenate([g, u], axis=1), d], axis=0)
+
+    step_of = (1, -1)
+    perms = [[(order[i], order[(i + t) % size]) for i in range(size)] for t in step_of]
+    held = [piece(way, pos) for way in range(2)]
+    for s in range(size - 1):
+        for way, t in enumerate(step_of):
+            came = lax.ppermute(held[way], axes, perms[way])
+            own = piece(way, lax.rem(pos - t * (s + 1) + size, size))
+            held[way] = (came.astype(F32) + own.astype(F32)).astype(BF16)
+    totals = [jnp.zeros(a.shape, F32) for a in (gate, up, down)]
+    for s in range(size):
+        for way, t in enumerate(step_of):
+            index = lax.rem(pos + t * (1 - s) + size, size)
+            now = held[way]
+            if s < size - 1:
+                held[way] = lax.ppermute(now, axes, perms[way])
+            for i, part in enumerate((now[:rows, :half], now[:rows, half:], now[rows:])):
+                totals[i] = lax.dynamic_update_slice(
+                    totals[i], part.astype(F32)[None, None], (way, index, 0, 0)
+                )
+    return [a.reshape(shape) for a, shape in zip(totals, shapes)]
 
 
 def body(
@@ -185,8 +228,8 @@
     y_two = lax.psum_scatter(
         partial_y.astype(BF16), "expert", scatter_dimension=0, tiled=True
     ).astype(F32)
-    total_gate, total_up, total_down = (
-        lax.psum(jnp.stack(g), ("context", "dp")).astype(F32) for g in (g_gate, g_up, g_down)
+    total_gate, total_up, total_down = ring_sum(
+        jnp.stack(g_gate), jnp.stack(g_up), jnp.stack(g_down)
     )
     outputs = (y_one + y_two).astype(BF16)[None]
 
@@ -196,7 +239,7 @@
     grad_logits = (
         own * (grad_weights - jnp.sum(own * grad_weights, axis=-1, keepdims=True))
     ).astype(BF16)
-    grad_router_w = t_dot(h_two, grad_logits)
+    grad_router_w = t_dot(grad_logits, h_two)
     grad_h_two = home[:, :width] + dot_t(grad_logits, w_router)
     grad_gain_two = jnp.sum(grad_h_two * normed_two, axis=0)
     grad_y_one = grad_final + norm_back(grad_h_two * gain_two, normed_two, inv_two)
@@ -246,16 +289,29 @@
     grad_inputs = grad_y_one + norm_back(grad_h_one * gain_one, normed_one, inv_one)
     grad_tokens = grad_inputs.astype(BF16)[None]
     everywhere = ("expert", "context", "dp")
-    total_o = lax.psum(grad_out_w.astype(BF16), everywhere).astype(F32)
-    total_q, total_k, total_v = (
+    small = jnp.concatenate(
+        [grad_router_w, grad_gain_one[None], grad_gain_two[None], jnp.zeros((14, width), F32)], axis=0
+    )
+    total_ors, total_q, total_k, total_v = (
         t.astype(F32)
         for t in lax.psum(
-            tuple(g.astype(BF16) for g in (grad_query_w, grad_key_w, grad_value_w)), everywhere
+            tuple(
+                g.astype(BF16)
+                for g in (
+                    jnp.concatenate([grad_out_w, small], axis=0),
+                    grad_query_w,
+                    grad_key_w,
+                    grad_value_w,
+                )
+            ),
+            everywhere,
         )
     )
-    total_g1, total_g2, total_r = lax.psum(
-        (grad_gain_one, grad_gain_two, grad_router_w), everywhere
-    )
+    mid = H * HD
+    total_o = total_ors[:mid]
+    total_r = total_ors[mid : mid + EXPERTS].T
+    total_g1 = total_ors[mid + EXPERTS]
+    total_g2 = total_ors[mid + EXPERTS + 1]
     return (
         outputs,
         grad_tokens,

time: 968 us -> 637 us (0.66)
  waiting for transfers between devices: 668 us -> 273 us
  blocking collectives: 45.5 us -> 5.37 us
  other arithmetic: 52.2 us -> 91.3 us
  local copies, waits for them, and re-layouts: 32.3 us -> 68.6 us
  starting transfers between devices: 0.75 us -> 32.8 us
  matrix products: 145 us -> 131 us
  between operations: 15.3 us -> 27 us
    psum x3 -> x1, waiting for transfers between devices: 592 us -> 89.7 us  [body(): lax.psum(tuple((g.astype(BF16) for g in (jnp.concatenate([grad_out_w, sma...]
    ppermute x0 -> x28, waiting for transfers between devices: none -> 167 us  [the longest x14 84.7 us: ring_sum(): came = lax.ppermute(held[way], axes, perms[way])]
    dynamic_update_slice x0 -> x33, other arithmetic: none -> 45.5 us  [ring_sum(): lax.dynamic_update_slice(totals[i], part.astype(F32)[None, None], (way, i...]
    psum x1 -> x0, blocking collectives: 40.1 us -> none  [body(): lax.psum((grad_gain_one, grad_gain_two, grad_router_w), everywhere)]
    ppermute x0 -> x28, starting transfers between devices: none -> 32.5 us  [the longest x14 16.5 us: ring_sum(): held[way] = lax.ppermute(now, axes, perms[way])]
    reduce_scatter x1, waiting for transfers between devices: 30.9 us -> 0.01 us  [body(): lax.psum_scatter(partial_y.astype(BF16), 'expert', scatter_dimension=0, t...]
    concatenate x0 -> x1, local copies, waits for them, and re-layouts: none -> 12.1 us  [body(): jnp.concatenate([grad_out_w, small], axis=0)]
    all_gather x1, waiting for transfers between devices: 11.5 us -> 0.01 us  [body(): h_all = lax.all_gather(h_two, 'expert', axis=0, tiled=True)]
  transfers between devices with their start and end apart: 9 -> 35, of which waited for: 8 -> 21; matrix products, arithmetic and copies ran while one was open for 13% -> 34% of each run, Pallas kernels for 0% -> 0%
where the time goes in v2:
time: 637 us; the launch traced here: 628 us
  waiting for transfers between devices  273 us (43%)
  matrix products  131 us (21%)
  other arithmetic  91.3 us (14%)
  local copies, waits for them, and re-layouts  68.6 us (11%)
  starting transfers between devices  32.8 us (5%)
  between operations  27 us (4%)
    psum x1, waiting for transfers between devices, body(): lax.psum(tuple((g.astype(BF16) for g in (jnp.concatenate([grad_out_w, sma...  89.7 us
    ppermute x14, waiting for transfers between devices, ring_sum(): came = lax.ppermute(held[way], axes, perms[way])  84.7 us
    ppermute x14, waiting for transfers between devices, ring_sum(): held[way] = lax.ppermute(now, axes, perms[way])  82.3 us
    dynamic_update_slice x33, other arithmetic, ring_sum(): lax.dynamic_update_slice(totals[i], part.astype(F32)[None, None], (way, i...  45.5 us
    dot_general x17, matrix products, dot_t(): lax.dot_general(a, b, (((1,), (1,)), ((), ())), preferred_element_type=F32)  44.3 us
    dot_general x17, matrix products, dot(): return jnp.dot(a, b, preferred_element_type=F32)  36.2 us
    dot_general x17, matrix products, t_dot(): lax.dot_general(a, b, (((0,), (0,)), ((), ())), preferred_element_type=F32)  26 us
    unnamed x242, local copies, waits for them, and re-layouts  24.6 us
  transfers between devices with their start and end apart: 35, of which 21 were waited for; matrix products, arithmetic and copies ran while one was open for 34% of the time, Pallas kernels for 0%

profile of v2, /device:TPU:0, one launch (start us, length us, event | category | flops | bytes accessed | tf_op | source)
XLA Modules:
  0.0 628.4 jit_solution(10185090696432636286)
XLA Ops:
  19.1 3.9 copy.123
  27.1 15.2 %all-gather.6.cloned.1.call-done = bf16[512,1024]{1,0:T(8,128)(2,1)} async-done(((bf16[256,1024]{1,0:T(8,128)(2,1)}), bf16[512,1024]{1,0:T(8,128)(2,1)}) %all-gather.6.cloned.1.call-update) | async-done | bytes 1048592 | tf_op jit(solution)/shard_map/all_gather | solution.py:149
  46.7 8.0 %fusion.204 = (f32[8,2,256]{2,1,0:T(2,128)}, f32[8,2,256,512]{2,3,1,0:T(8,128)}) fusion(pred[256,512]{0,1:T(8,128)(4,1)S(1)} %copy-done.83, bf16[512,8,64,1]{0,2,3,1:T(8,128)(2,1)S(1)} %bitcast.681, bf16[256,8,2,32]{0,3,2,1:T(8,128)(2,1)} %bitcast.691, bf16[256,8,2,32]{0,3,2,1:T(8,128)(2,1)S(1)} %bitcast.689), kind=kOutput, calls=%fused_computation.447 | convolution fusion | flops 277873152 | bytes 9584640 | tf_op jit(solution)/shard_map/sub | solution.py:163
  54.7 4.3 fusion.74
  74.0 5.4 all-gather
  79.5 4.6 fusion.16
  103.1 3.8 multiply_convert_fusion.1
  106.9 3.9 multiply_convert_fusion.3
  127.9 3.5 fusion.129
  134.7 9.2 %add_convert_fusion = bf16[1024,1024]{0,1:T(8,128)(2,1)S(1)} fusion(f32[1024,1024]{0,1:T(8,128)S(1)} %fusion.96, f32[1024,1024]{0,1:T(8,128)S(1)} %fusion.107, f32[1024,1024]{0,1:T(8,128)S(1)} %fusion.103, f32[1024,1024]{0,1:T(8,128)} %fusion.118, f32[1024,1024]{0,1:T(8,128)} %fusion.114, f32[1024,1024]{0,1:T(8,128)} %fusion.129, f32[1024,1024]{0,1:T(8,128)} %fusion.125, ...), kind=kOutput, calls=%fused_computation.9 | convolution fusion | flops 1082130432 | bytes 33554432 | tf_op jit(solution)/shard_map/dot_general | solution.py:60
  183.1 3.6 collective-permute-done
  189.5 10.0 %collective-permute-done.7 = bf16[384,1024]{1,0:T(8,128)(2,1)S(1)} collective-permute-done((bf16[384,1024]{1,0:T(8,128)(2,1)S(1)}, bf16[384,1024]{1,0:T(8,128)(2,1)S(1)}, u32[]{:S(2)}, u32[]{:S(2)}) %collective-permute-start.7) | collective-permute-done | bytes 786464 | tf_op jit(solution)/shard_map/ppermute | solution.py:93
  210.5 9.2 %collective-permute-done.8 = bf16[384,1024]{1,0:T(8,128)(2,1)} collective-permute-done((bf16[384,1024]{1,0:T(8,128)(2,1)}, bf16[384,1024]{1,0:T(8,128)(2,1)}, u32[]{:S(2)}, u32[]{:S(2)}) %collective-permute-start.8) | collective-permute-done | bytes 786464 | tf_op jit(solution)/shard_map/ppermute | solution.py:93
  221.7 5.2 collective-permute-done.2
  228.9 10.1 %collective-permute-done.9 = bf16[384,1024]{1,0:T(8,128)(2,1)S(1)} collective-permute-done((bf16[384,1024]{1,0:T(8,128)(2,1)S(1)}, bf16[384,1024]{1,0:T(8,128)(2,1)S(1)}, u32[]{:S(2)}, u32[]{:S(2)}) %collective-permute-start.9) | collective-permute-done | bytes 786464 | tf_op jit(solution)/shard_map/ppermute | solution.py:93
  239.8 4.6 collective-permute-done.3
  247.4 8.9 %collective-permute-done.10 = bf16[384,1024]{1,0:T(8,128)(2,1)S(1)} collective-permute-done((bf16[384,1024]{1,0:T(8,128)(2,1)S(1)}, bf16[384,1024]{1,0:T(8,128)(2,1)S(1)}, u32[]{:S(2)}, u32[]{:S(2)}) %collective-permute-start.10) | collective-permute-done | bytes 786464 | tf_op jit(solution)/shard_map/ppermute | solution.py:93
  266.4 7.5 %collective-permute-done.11 = bf16[384,1024]{1,0:T(8,128)(2,1)} collective-permute-done((bf16[384,1024]{1,0:T(8,128)(2,1)}, bf16[384,1024]{1,0:T(8,128)(2,1)}, u32[]{:S(2)}, u32[]{:S(2)}) %collective-permute-start.11) | collective-permute-done | bytes 786464 | tf_op jit(solution)/shard_map/ppermute | solution.py:93
  286.2 4.9 fusion.1
  291.2 4.8 fusion.78
  296.0 4.5 fusion.3
  320.8 19.4 %collective-permute-done.6 = bf16[384,1024]{1,0:T(8,128)(2,1)S(1)} collective-permute-done((bf16[384,1024]{1,0:T(8,128)(2,1)S(1)}, bf16[384,1024]{1,0:T(8,128)(2,1)S(1)}, u32[]{:S(2)}, u32[]{:S(2)}) %collective-permute-start.6) | collective-permute-done | bytes 786464 | tf_op jit(solution)/shard_map/ppermute | solution.py:93
  340.8 4.5 broadcast.329.clone
  348.2 4.5 broadcast.329.clone.1
  353.5 4.5 broadcast_in_dim.479
  378.9 12.1 %concatenate.148 = bf16[1056,1024]{1,0:T(8,128)(2,1)} concatenate(bf16[1024,1024]{1,0:T(8,128)(2,1)} %convolution_convert_fusion.1, bf16[16,1024]{1,0:T(8,128)(2,1)S(1)} %copy-done.82, bf16[1,1024]{1,0:T(2,128)(2,1)S(1)} %broadcast_in_dim.412, bf16[1,1024]{1,0:T(2,128)(2,1)S(1)} %broadcast_in_dim.413, bf16[14,1024]{1,0:T(8,128)(2,1)S(1)} %broadcast_in_dim.414), dimensions={0} | concatenate | bytes 4325376 | tf_op jit(solution)/shard_map/concatenate | solution.py:301
  404.0 19.9 %collective-permute-done.18 = bf16[384,1024]{1,0:T(8,128)(2,1)S(1)} collective-permute-done((bf16[384,1024]{1,0:T(8,128)(2,1)}, bf16[384,1024]{1,0:T(8,128)(2,1)S(1)}, u32[]{:S(2)}, u32[]{:S(2)}) %collective-permute-start.18) | collective-permute-done | bytes 786464 | tf_op jit(solution)/shard_map/ppermute | solution.py:102
  430.5 27.9 %collective-permute-done.20 = bf16[384,1024]{1,0:T(8,128)(2,1)S(1)} collective-permute-done((bf16[384,1024]{1,0:T(8,128)(2,1)S(1)}, bf16[384,1024]{1,0:T(8,128)(2,1)S(1)}, u32[]{:S(2)}, u32[]{:S(2)}) %collective-permute-start.20) | collective-permute-done | bytes 786464 | tf_op jit(solution)/shard_map/ppermute | solution.py:102
  465.2 19.2 %collective-permute-done.22 = bf16[384,1024]{1,0:T(8,128)(2,1)} collective-permute-done((bf16[384,1024]{1,0:T(8,128)(2,1)S(1)}, bf16[384,1024]{1,0:T(8,128)(2,1)}, u32[]{:S(2)}, u32[]{:S(2)}) %collective-permute-start.22) | collective-permute-done | bytes 786464 | tf_op jit(solution)/shard_map/ppermute | solution.py:102
  495.4 89.7 %all-reduce.3.cloned.1.call-done = (bf16[1056,1024]{1,0:T(8,128)(2,1)}, bf16[1024,1024]{1,0:T(8,128)(2,1)}, bf16[1024,512]{1,0:T(8,128)(2,1)}, bf16[1024,512]{1,0:T(8,128)(2,1)}) async-done(((bf16[1056,1024]{1,0:T(8,128)(2,1)}, bf16[1024,1024]{1,0:T(8,128)(2,1)}, bf16[1024,512]{1,0:T(8,128)(2,1)}, bf16[1024,512]{1,0:T(8,128)(2,1)}), (bf16[1056,1024]{1,0:T(8,128)(2,1)}, bf16[1024,1024]{1,0:T(8,128)(2,1)}, ...) | async-done | bytes 6357008 | tf_op jit(solution)/shard_map/psum | solution.py:297
  585.1 4.2 slice.422
  605.7 11.8 %collective-permute-done.26 = bf16[384,1024]{1,0:T(8,128)(2,1)S(1)} collective-permute-done((bf16[384,1024]{1,0:T(8,128)(2,1)}, bf16[384,1024]{1,0:T(8,128)(2,1)S(1)}, u32[]{:S(2)}, u32[]{:S(2)}) %collective-permute-start.26) | collective-permute-done | bytes 786464 | tf_op jit(solution)/shard_map/ppermute | solution.py:102
  (466 shorter events, 248.7 us)
Async XLA Ops:
  7.2 35.2 %all-gather.6.cloned.1.call-start = ((), (), s32[]{:S(2)}) async-start(), calls=%async_computation.3 | async-start | bytes 1572864 | tf_op jit(solution)/shard_map/all_gather | solution.py:149
  18.2 61.3 %all-gather.10.cloned.1.call-start = ((), (), s32[]{:S(2)}) async-start(), calls=%async_computation.8 | async-start | bytes 2621440 | tf_op jit(solution)/shard_map/all_gather | solution.py:133
  18.9 73.0 %all-gather.8.cloned.1.call-start = ((), (), s32[]{:S(2)}) async-start(), calls=%async_computation.4 | async-start | bytes 2621440 | tf_op jit(solution)/shard_map/all_gather | solution.py:176
  62.1 214.5 %reduce-scatter.6.cloned.1.call-start = ((), (), s32[]{:S(2)}) async-start(), calls=%async_computation.6 | async-start | bytes 2949120 | tf_op jit(solution)/shard_map/reduce_scatter | solution.py:227
  146.8 134.0 %reduce-scatter.4.cloned.1.call-start = ((), (), s32[]{:S(2)}) async-start(), calls=%async_computation.5 | async-start | bytes 2621440 | tf_op jit(solution)/shard_map/reduce_scatter | solution.py:228
  166.5 20.2 %collective-permute-start = (bf16[384,1024]{1,0:T(8,128)(2,1)S(1)}, bf16[384,1024]{1,0:T(8,128)(2,1)S(1)}, u32[]{:S(2)}, u32[]{:S(2)}) collective-permute-start(bf16[384,1024]{1,0:T(8,128)(2,1)S(1)} %pad_maximum_fusion.7), channel_id=1, source_target_pairs={{0,1},{1,2},{2,3},{3,7},{7,6},{6,5},{5,4},{4,0},{8,9},{9,10},{10,1... | collective-permute-start | bytes 2359304 | tf_op jit(solution)/shard_map/ppermute | solution.py:93
  179.9 19.5 %collective-permute-start.7 = (bf16[384,1024]{1,0:T(8,128)(2,1)S(1)}, bf16[384,1024]{1,0:T(8,128)(2,1)S(1)}, u32[]{:S(2)}, u32[]{:S(2)}) collective-permute-start(bf16[384,1024]{1,0:T(8,128)(2,1)S(1)} %pad_maximum_fusion.8), channel_id=1, source_target_pairs={{0,4},{1,0},{2,1},{3,2},{7,3},{6,7},{5,6},{4,5},{8,12},{9,8},{10,9... | collective-permute-start | bytes 2359304 | tf_op jit(solution)/shard_map/ppermute | solution.py:93
  187.8 19.3 %collective-permute-start.1 = (bf16[384,1024]{1,0:T(8,128)(2,1)}, bf16[384,1024]{1,0:T(8,128)(2,1)}, u32[]{:S(2)}, u32[]{:S(2)}) collective-permute-start(bf16[384,1024]{1,0:T(8,128)(2,1)} %add_convert_fusion.15), channel_id=1, source_target_pairs={{0,1},{1,2},{2,3},{3,7},{7,6},{6,5},{5,4},{4,0},{8,9},{9,10},{10,1... | collective-permute-start | bytes 2359304 | tf_op jit(solution)/shard_map/ppermute | solution.py:93
  200.6 19.1 %collective-permute-start.8 = (bf16[384,1024]{1,0:T(8,128)(2,1)}, bf16[384,1024]{1,0:T(8,128)(2,1)}, u32[]{:S(2)}, u32[]{:S(2)}) collective-permute-start(bf16[384,1024]{1,0:T(8,128)(2,1)} %add_convert_fusion.8), channel_id=1, source_target_pairs={{0,4},{1,0},{2,1},{3,2},{7,3},{6,7},{5,6},{4,5},{8,12},{9,8},{10,9... | collective-permute-start | bytes 2359304 | tf_op jit(solution)/shard_map/ppermute | solution.py:93
  204.2 169.5 %reduce-scatter.8.cloned.1.call-start = ((), (), s32[]{:S(2)}) async-start(), calls=%async_computation.7 | async-start | bytes 1572864 | tf_op jit(solution)/shard_map/reduce_scatter | solution.py:259
  208.6 18.2 %collective-permute-start.2 = (bf16[384,1024]{1,0:T(8,128)(2,1)S(1)}, bf16[384,1024]{1,0:T(8,128)(2,1)S(1)}, u32[]{:S(2)}, u32[]{:S(2)}) collective-permute-start(bf16[384,1024]{1,0:T(8,128)(2,1)S(1)} %add_convert_fusion.14), channel_id=1, source_target_pairs={{0,1},{1,2},{2,3},{3,7},{7,6},{6,5},{5,4},{4,0},{8,9},{9,10},{10,1... | collective-permute-start | bytes 2359304 | tf_op jit(solution)/shard_map/ppermute | solution.py:93
  221.2 17.9 %collective-permute-start.9 = (bf16[384,1024]{1,0:T(8,128)(2,1)S(1)}, bf16[384,1024]{1,0:T(8,128)(2,1)S(1)}, u32[]{:S(2)}, u32[]{:S(2)}) collective-permute-start(bf16[384,1024]{1,0:T(8,128)(2,1)S(1)} %add_convert_fusion.7), channel_id=1, source_target_pairs={{0,4},{1,0},{2,1},{3,2},{7,3},{6,7},{5,6},{4,5},{8,12},{9,8},{10,9... | collective-permute-start | bytes 2359304 | tf_op jit(solution)/shard_map/ppermute | solution.py:93
  227.2 17.3 %collective-permute-start.3 = (bf16[384,1024]{1,0:T(8,128)(2,1)S(1)}, bf16[384,1024]{1,0:T(8,128)(2,1)S(1)}, u32[]{:S(2)}, u32[]{:S(2)}) collective-permute-start(bf16[384,1024]{1,0:T(8,128)(2,1)S(1)} %add_convert_fusion.13), channel_id=1, source_target_pairs={{0,1},{1,2},{2,3},{3,7},{7,6},{6,5},{5,4},{4,0},{8,9},{9,10},{10,1... | collective-permute-start | bytes 2359304 | tf_op jit(solution)/shard_map/ppermute | solution.py:93
  264.6 47.0 %collective-permute-start.5 = (bf16[384,1024]{1,0:T(8,128)(2,1)}, bf16[384,1024]{1,0:T(8,128)(2,1)}, u32[]{:S(2)}, u32[]{:S(2)}) collective-permute-start(bf16[384,1024]{1,0:T(8,128)(2,1)} %add_convert_fusion.11), channel_id=1, source_target_pairs={{0,1},{1,2},{2,3},{3,7},{7,6},{6,5},{5,4},{4,0},{8,9},{9,10},{10,1... | collective-permute-start | bytes 2359304 | tf_op jit(solution)/shard_map/ppermute | solution.py:93
  276.2 38.9 %collective-permute-start.12 = (bf16[384,1024]{1,0:T(8,128)(2,1)}, bf16[384,1024]{1,0:T(8,128)(2,1)}, u32[]{:S(2)}, u32[]{:S(2)}) collective-permute-start(bf16[384,1024]{1,0:T(8,128)(2,1)} %add_convert_fusion.4), channel_id=1, source_target_pairs={{0,4},{1,0},{2,1},{3,2},{7,3},{6,7},{5,6},{4,5},{8,12},{9,8},{10,9... | collective-permute-start | bytes 2359304 | tf_op jit(solution)/shard_map/ppermute | solution.py:93
  305.9 279.2 %all-reduce.3.cloned.1.call-start = ((), (), s32[]{:S(2)}) async-start(), calls=%async_computation.9 | async-start | bytes 12713984 | tf_op jit(solution)/shard_map/psum | solution.py:297
  313.3 26.9 %collective-permute-start.6 = (bf16[384,1024]{1,0:T(8,128)(2,1)S(1)}, bf16[384,1024]{1,0:T(8,128)(2,1)S(1)}, u32[]{:S(2)}, u32[]{:S(2)}) collective-permute-start(bf16[384,1024]{1,0:T(8,128)(2,1)S(1)} %add_convert_fusion.10), channel_id=1, source_target_pairs={{0,1},{1,2},{2,3},{3,7},{7,6},{6,5},{5,4},{4,0},{8,9},{9,10},{10,1... | collective-permute-start | bytes 2359304 | tf_op jit(solution)/shard_map/ppermute | solution.py:93
  316.5 24.0 %collective-permute-start.13 = (bf16[384,1024]{1,0:T(8,128)(2,1)S(1)}, bf16[384,1024]{1,0:T(8,128)(2,1)S(1)}, u32[]{:S(2)}, u32[]{:S(2)}) collective-permute-start(bf16[384,1024]{1,0:T(8,128)(2,1)S(1)} %add_convert_fusion.3), channel_id=1, source_target_pairs={{0,4},{1,0},{2,1},{3,2},{7,3},{6,7},{5,6},{4,5},{8,12},{9,8},{10,9... | collective-permute-start | bytes 2359304 | tf_op jit(solution)/shard_map/ppermute | solution.py:93
  340.5 20.2 %collective-permute-start.14 = (bf16[384,1024]{1,0:T(8,128)(2,1)S(1)}, bf16[384,1024]{1,0:T(8,128)(2,1)}, u32[]{:S(2)}, u32[]{:S(2)}) collective-permute-start(bf16[384,1024]{1,0:T(8,128)(2,1)S(1)} %add_convert_fusion.9), channel_id=1, source_target_pairs={{0,1},{1,2},{2,3},{3,7},{7,6},{6,5},{5,4},{4,0},{8,9},{9,10},{10,1... | collective-permute-start | bytes 2359304 | tf_op jit(solution)/shard_map/ppermute | solution.py:102
  346.2 17.1 %collective-permute-start.15 = (bf16[384,1024]{1,0:T(8,128)(2,1)S(1)}, bf16[384,1024]{1,0:T(8,128)(2,1)}, u32[]{:S(2)}, u32[]{:S(2)}) collective-permute-start(bf16[384,1024]{1,0:T(8,128)(2,1)S(1)} %add_convert_fusion.2), channel_id=1, source_target_pairs={{0,4},{1,0},{2,1},{3,2},{7,3},{6,7},{5,6},{4,5},{8,12},{9,8},{10,9... | collective-permute-start | bytes 2359304 | tf_op jit(solution)/shard_map/ppermute | solution.py:102
  360.7 33.3 %collective-permute-start.16 = (bf16[384,1024]{1,0:T(8,128)(2,1)}, bf16[384,1024]{1,0:T(8,128)(2,1)}, u32[]{:S(2)}, u32[]{:S(2)}) collective-permute-start(bf16[384,1024]{1,0:T(8,128)(2,1)} %collective-permute-done.14), channel_id=1, source_target_pairs={{0,1},{1,2},{2,3},{3,7},{7,6},{6,5},{5,4},{4,0},{8,9},{9,10},{10,1... | collective-permute-start | bytes 2359304 | tf_op jit(solution)/shard_map/ppermute | solution.py:102
  363.3 30.8 %collective-permute-start.17 = (bf16[384,1024]{1,0:T(8,128)(2,1)}, bf16[384,1024]{1,0:T(8,128)(2,1)}, u32[]{:S(2)}, u32[]{:S(2)}) collective-permute-start(bf16[384,1024]{1,0:T(8,128)(2,1)} %collective-permute-done.15), channel_id=1, source_target_pairs={{0,4},{1,0},{2,1},{3,2},{7,3},{6,7},{5,6},{4,5},{8,12},{9,8},{10,9... | collective-permute-start | bytes 2359304 | tf_op jit(solution)/shard_map/ppermute | solution.py:102
  394.0 29.9 %collective-permute-start.18 = (bf16[384,1024]{1,0:T(8,128)(2,1)}, bf16[384,1024]{1,0:T(8,128)(2,1)S(1)}, u32[]{:S(2)}, u32[]{:S(2)}) collective-permute-start(bf16[384,1024]{1,0:T(8,128)(2,1)} %collective-permute-done.16), channel_id=1, source_target_pairs={{0,1},{1,2},{2,3},{3,7},{7,6},{6,5},{5,4},{4,0},{8,9},{9,10},{10,1... | collective-permute-start | bytes 2359304 | tf_op jit(solution)/shard_map/ppermute | solution.py:102
  394.1 32.5 %collective-permute-start.19 = (bf16[384,1024]{1,0:T(8,128)(2,1)}, bf16[384,1024]{1,0:T(8,128)(2,1)S(1)}, u32[]{:S(2)}, u32[]{:S(2)}) collective-permute-start(bf16[384,1024]{1,0:T(8,128)(2,1)} %collective-permute-done.17), channel_id=1, source_target_pairs={{0,4},{1,0},{2,1},{3,2},{7,3},{6,7},{5,6},{4,5},{8,12},{9,8},{10,9... | collective-permute-start | bytes 2359304 | tf_op jit(solution)/shard_map/ppermute | solution.py:102
  423.9 34.5 %collective-permute-start.20 = (bf16[384,1024]{1,0:T(8,128)(2,1)S(1)}, bf16[384,1024]{1,0:T(8,128)(2,1)S(1)}, u32[]{:S(2)}, u32[]{:S(2)}) collective-permute-start(bf16[384,1024]{1,0:T(8,128)(2,1)S(1)} %collective-permute-done.18), channel_id=1, source_target_pairs={{0,1},{1,2},{2,3},{3,7},{7,6},{6,5},{5,4},{4,0},{8,9},{9,10},{10,1... | collective-permute-start | bytes 2359304 | tf_op jit(solution)/shard_map/ppermute | solution.py:102
  426.6 34.4 %collective-permute-start.21 = (bf16[384,1024]{1,0:T(8,128)(2,1)S(1)}, bf16[384,1024]{1,0:T(8,128)(2,1)S(1)}, u32[]{:S(2)}, u32[]{:S(2)}) collective-permute-start(bf16[384,1024]{1,0:T(8,128)(2,1)S(1)} %collective-permute-done.19), channel_id=1, source_target_pairs={{0,4},{1,0},{2,1},{3,2},{7,3},{6,7},{5,6},{4,5},{8,12},{9,8},{10,9... | collective-permute-start | bytes 2359304 | tf_op jit(solution)/shard_map/ppermute | solution.py:102
  458.4 26.0 %collective-permute-start.22 = (bf16[384,1024]{1,0:T(8,128)(2,1)S(1)}, bf16[384,1024]{1,0:T(8,128)(2,1)}, u32[]{:S(2)}, u32[]{:S(2)}) collective-permute-start(bf16[384,1024]{1,0:T(8,128)(2,1)S(1)} %collective-permute-done.20), channel_id=1, source_target_pairs={{0,1},{1,2},{2,3},{3,7},{7,6},{6,5},{5,4},{4,0},{8,9},{9,10},{10,1... | collective-permute-start | bytes 2359304 | tf_op jit(solution)/shard_map/ppermute | solution.py:102
  461.0 26.5 %collective-permute-start.23 = (bf16[384,1024]{1,0:T(8,128)(2,1)S(1)}, bf16[384,1024]{1,0:T(8,128)(2,1)}, u32[]{:S(2)}, u32[]{:S(2)}) collective-permute-start(bf16[384,1024]{1,0:T(8,128)(2,1)S(1)} %collective-permute-done.21), channel_id=1, source_target_pairs={{0,4},{1,0},{2,1},{3,2},{7,3},{6,7},{5,6},{4,5},{8,12},{9,8},{10,9... | collective-permute-start | bytes 2359304 | tf_op jit(solution)/shard_map/ppermute | solution.py:102
  484.4 113.5 %collective-permute-start.24 = (bf16[384,1024]{1,0:T(8,128)(2,1)}, bf16[384,1024]{1,0:T(8,128)(2,1)}, u32[]{:S(2)}, u32[]{:S(2)}) collective-permute-start(bf16[384,1024]{1,0:T(8,128)(2,1)} %collective-permute-done.22), channel_id=1, source_target_pairs={{0,1},{1,2},{2,3},{3,7},{7,6},{6,5},{5,4},{4,0},{8,9},{9,10},{10,1... | collective-permute-start | bytes 2359304 | tf_op jit(solution)/shard_map/ppermute | solution.py:102
  487.5 111.6 %collective-permute-start.25 = (bf16[384,1024]{1,0:T(8,128)(2,1)}, bf16[384,1024]{1,0:T(8,128)(2,1)S(1)}, u32[]{:S(2)}, u32[]{:S(2)}) collective-permute-start(bf16[384,1024]{1,0:T(8,128)(2,1)} %collective-permute-done.23), channel_id=1, source_target_pairs={{0,4},{1,0},{2,1},{3,2},{7,3},{6,7},{5,6},{4,5},{8,12},{9,8},{10,9... | collective-permute-start | bytes 2359304 | tf_op jit(solution)/shard_map/ppermute | solution.py:102
  597.8 19.7 %collective-permute-start.26 = (bf16[384,1024]{1,0:T(8,128)(2,1)}, bf16[384,1024]{1,0:T(8,128)(2,1)S(1)}, u32[]{:S(2)}, u32[]{:S(2)}) collective-permute-start(bf16[384,1024]{1,0:T(8,128)(2,1)} %collective-permute-done.24), channel_id=1, source_target_pairs={{0,1},{1,2},{2,3},{3,7},{7,6},{6,5},{5,4},{4,0},{8,9},{9,10},{10,1... | collective-permute-start | bytes 2359304 | tf_op jit(solution)/shard_map/ppermute | solution.py:102
  599.2 20.3 %collective-permute-start.27 = (bf16[384,1024]{1,0:T(8,128)(2,1)S(1)}, bf16[384,1024]{1,0:T(8,128)(2,1)S(1)}, u32[]{:S(2)}, u32[]{:S(2)}) collective-permute-start(bf16[384,1024]{1,0:T(8,128)(2,1)S(1)} %collective-permute-done.25), channel_id=1, source_target_pairs={{0,4},{1,0},{2,1},{3,2},{7,3},{6,7},{5,6},{4,5},{8,12},{9,8},{10,9... | collective-permute-start | bytes 2359304 | tf_op jit(solution)/shard_map/ppermute | solution.py:102
  (121 other events, 1100.8 us)
Sparse Core Ops, SparseCore 0:
  18.3 24.0 all-gather.5
  43.9 22.5 all-gather.9
  68.7 22.8 all-gather.7
  146.9 33.0 reduce-scatter.5
  204.3 31.5 reduce-scatter.3
  306.0 30.7 reduce-scatter.7
  394.1 190.9 all-reduce.2

commit v3 on v2

--- a/solution.py
+++ b/solution.py
@@ -225,8 +225,9 @@
         axis=1,
     )
     home = lax.psum_scatter(packed, "expert", scatter_dimension=0, tiled=True).astype(F32)
+    home, later_y = lax.optimization_barrier((home, partial_y.astype(BF16)))
     y_two = lax.psum_scatter(
-        partial_y.astype(BF16), "expert", scatter_dimension=0, tiled=True
+        later_y, "expert", scatter_dimension=0, tiled=True
     ).astype(F32)
     total_gate, total_up, total_down = ring_sum(
         jnp.stack(g_gate), jnp.stack(g_up), jnp.stack(g_down)
@@ -288,30 +289,26 @@
     grad_gain_one = jnp.sum(grad_h_one * normed_one, axis=0)
     grad_inputs = grad_y_one + norm_back(grad_h_one * gain_one, normed_one, inv_one)
     grad_tokens = grad_inputs.astype(BF16)[None]
-    everywhere = ("expert", "context", "dp")
-    small = jnp.concatenate(
-        [grad_router_w, grad_gain_one[None], grad_gain_two[None], jnp.zeros((14, width), F32)], axis=0
-    )
-    total_ors, total_q, total_k, total_v = (
-        t.astype(F32)
-        for t in lax.psum(
-            tuple(
-                g.astype(BF16)
-                for g in (
-                    jnp.concatenate([grad_out_w, small], axis=0),
-                    grad_query_w,
-                    grad_key_w,
-                    grad_value_w,
-                )
-            ),
-            everywhere,
-        )
-    )
-    mid = H * HD
-    total_o = total_ors[:mid]
-    total_r = total_ors[mid : mid + EXPERTS].T
-    total_g1 = total_ors[mid + EXPERTS]
-    total_g2 = total_ors[mid + EXPERTS + 1]
+    mid, kvw = H * HD, KV * HD
+    small = jnp.concatenate([grad_router_w, grad_gain_one[None], grad_gain_two[None]], axis=0)
+    small = jnp.pad(small, ((0, 64 - EXPERTS - 2), (0, 2 * mid)))
+    packed_grads = jnp.concatenate(
+        [
+            jnp.concatenate([grad_query_w, grad_key_w, grad_value_w, grad_out_w], axis=1).astype(BF16),
+            small.astype(BF16),
+        ],
+        axis=0,
+    )
+    share = lax.psum_scatter(packed_grads, "expert", scatter_dimension=0, tiled=True)
+    share = lax.psum(share, ("context", "dp"))
+    total = lax.all_gather(share, "expert", axis=0, tiled=True)
+    total_q = total[:width, :mid].astype(F32)
+    total_k = total[:width, mid : mid + kvw].astype(F32)
+    total_v = total[:width, mid + kvw : mid + 2 * kvw].astype(F32)
+    total_o = total[:width, 2 * mid :].astype(F32)
+    total_r = total[width : width + EXPERTS, :width].astype(F32).T
+    total_g1 = total[width + EXPERTS, :width].astype(F32)
+    total_g2 = total[width + EXPERTS + 1, :width].astype(F32)
     return (
         outputs,
         grad_tokens,

time: 637 us -> 716 us (1.12)
  waiting for transfers between devices: 273 us -> 331 us
  other arithmetic: 91.3 us -> 106 us
    ppermute x14, waiting for transfers between devices: 82.3 us -> 54 us  [ring_sum(): held[way] = lax.ppermute(now, axes, perms[way])]
    reduce_scatter x1, waiting for transfers between devices: 0.01 us -> 26.1 us  [body(): lax.psum_scatter(later_y, 'expert', scatter_dimension=0, tiled=True)]
    ppermute x14, waiting for transfers between devices: 84.7 us -> 110 us  [ring_sum(): came = lax.ppermute(held[way], axes, perms[way])]
    reduce_scatter x1, waiting for transfers between devices: 0.01 us -> 24.2 us  [body(): lax.psum_scatter(packed, 'expert', scatter_dimension=0, tiled=True)]
    unnamed x242 -> x158, local copies, waits for them, and re-layouts: 24.6 us -> 37.7 us
    concatenate x1, local copies, waits for them, and re-layouts: 12.1 us -> 0.19 us  [body(): jnp.concatenate([grad_router_w, grad_gain_one[None], grad_gain_two[None]]...]
    all_gather x1, waiting for transfers between devices: 0.01 us -> 11.1 us  [body(): h_all = lax.all_gather(h_two, 'expert', axis=0, tiled=True)]
    reduce_scatter x1, waiting for transfers between devices: 0.01 us -> 10.2 us  [body(): lax.psum_scatter(jnp.concatenate([grad_keys.reshape(seq_rows, KV * HD), g...]
  transfers between devices with their start and end apart: 35 -> 37, of which waited for: 21 -> 28; matrix products, arithmetic and copies ran while one was open for 34% -> 25% of each run, Pallas kernels for 0% -> 0%
where the time goes in v3:
time: 716 us; the launch traced here: 706 us
  waiting for transfers between devices  331 us (46%)
  matrix products  134 us (19%)
  other arithmetic  106 us (15%)
  local copies, waits for them, and re-layouts  67.2 us (9%)
  starting transfers between devices  34.8 us (5%)
  between operations  26.8 us (4%)
    ppermute x14, waiting for transfers between devices, ring_sum(): came = lax.ppermute(held[way], axes, perms[way])  110 us
    psum x1, waiting for transfers between devices, body(): share = lax.psum(share, ('context', 'dp'))  80.1 us
    ppermute x14, waiting for transfers between devices, ring_sum(): held[way] = lax.ppermute(now, axes, perms[way])  54 us
    dynamic_update_slice x33, other arithmetic, ring_sum(): lax.dynamic_update_slice(totals[i], part.astype(F32)[None, None], (way, i...  47.5 us
    dot_general x17, matrix products, dot_t(): lax.dot_general(a, b, (((1,), (1,)), ((), ())), preferred_element_type=F32)  46 us
    dot_general x17, matrix products, dot(): return jnp.dot(a, b, preferred_element_type=F32)  37.8 us
    unnamed x158, local copies, waits for them, and re-layouts  37.7 us
    reduce_scatter x1, waiting for transfers between devices, body(): lax.psum_scatter(later_y, 'expert', scatter_dimension=0, tiled=True)  26.1 us
  transfers between devices with their start and end apart: 37, of which 28 were waited for; matrix products, arithmetic and copies ran while one was open for 25% of the time, Pallas kernels for 0%

profile of v3, /device:TPU:0, one launch (start us, length us, event | category | flops | bytes accessed | tf_op | source)
XLA Modules:
  0.0 706.3 jit_solution(17590889053926241335)
XLA Ops:
  25.6 15.1 %all-gather.7.cloned.1.call-done = bf16[512,1024]{1,0:T(8,128)(2,1)} async-done(((bf16[256,1024]{1,0:T(8,128)(2,1)}), bf16[512,1024]{1,0:T(8,128)(2,1)}) %all-gather.7.cloned.1.call-update) | async-done | bytes 1048592 | tf_op jit(solution)/shard_map/all_gather | solution.py:149
  45.0 7.3 %fusion.205 = (f32[8,2,256]{2,1,0:T(2,128)S(1)}, f32[8,2,256,512]{2,3,1,0:T(8,128)}) fusion(pred[256,512]{0,1:T(8,128)(4,1)} %broadcast_compare_fusion, bf16[512,8,64,1]{0,2,3,1:T(8,128)(2,1)S(1)} %bitcast.682, bf16[256,8,2,32]{0,3,2,1:T(8,128)(2,1)} %bitcast.692, bf16[256,8,2,32]{0,3,2,1:T(8,128)(2,1)} %bitcast.690), kind=kOutput, calls=%fused_computation.456 | convolution fusion | flops 277873152 | bytes 9584640 | tf_op jit(solution)/shard_map/sub | solution.py:163
  60.6 5.6 all-gather.1
  66.4 4.6 fusion.18
  78.8 11.1 %all-gather.9.cloned.1.call-done = bf16[1024,1024]{0,1:T(8,128)(2,1)} async-done(((bf16[256,1024]{0,1:T(8,128)(2,1)}), bf16[1024,1024]{0,1:T(8,128)(2,1)}) %all-gather.9.cloned.1.call-update) | async-done | bytes 2097168 | tf_op jit(solution)/shard_map/all_gather | solution.py:176
  132.6 9.2 %add_convert_fusion.1 = bf16[1024,1024]{0,1:T(8,128)(2,1)S(1)} fusion(f32[1024,1024]{0,1:T(8,128)S(1)} %fusion.93, f32[1024,1024]{0,1:T(8,128)S(1)} %fusion.102, f32[1024,1024]{0,1:T(8,128)S(1)} %fusion.106, f32[1024,1024]{0,1:T(8,128)} %fusion.113, f32[1024,1024]{0,1:T(8,128)} %fusion.117, f32[1024,1024]{0,1:T(8,128)} %fusion.124, ...), kind=kOutput, calls=%fused_computation.13 | convolution fusion | flops 1082130432 | bytes 33554432 | tf_op jit(solution)/shard_map/dot_general | solution.py:60
  154.4 24.2 %reduce-scatter.7.cloned.1.call-done = bf16[256,1152]{0,1:T(8,128)(2,1)} async-done(((bf16[1024,1152]{0,1:T(8,128)(2,1)}), bf16[256,1152]{0,1:T(8,128)(2,1)}) %reduce-scatter.7.cloned.1.call-update) | async-done | bytes 589840 | tf_op jit(solution)/shard_map/reduce_scatter | solution.py:227
  187.0 26.1 %reduce-scatter.9.cloned.1.call-done = bf16[256,1024]{0,1:T(8,128)(2,1)} async-done(((bf16[1024,1024]{0,1:T(8,128)(2,1)}), bf16[256,1024]{0,1:T(8,128)(2,1)}) %reduce-scatter.9.cloned.1.call-update) | async-done | bytes 524304 | tf_op jit(solution)/shard_map/reduce_scatter | solution.py:229
  219.9 4.9 fusion.2
  224.8 4.8 fusion.80
  247.4 10.2 %reduce-scatter.11.cloned.1.call-done = bf16[256,1024]{0,1:T(8,128)(2,1)} async-done(((bf16[512,1024]{0,1:T(8,128)(2,1)}), bf16[256,1024]{0,1:T(8,128)(2,1)}) %reduce-scatter.11.cloned.1.call-update) | async-done | bytes 524304 | tf_op jit(solution)/shard_map/reduce_scatter | solution.py:260
  263.7 7.0 fusion.5
  270.7 10.1 %copy.183 = bf16[1088,3072]{1,0:T(8,128)(2,1)} copy(bf16[1088,3072]{0,1:T(8,128)(2,1)} %fusion.5) | data formatting | bytes 13369344
  324.3 9.2 %collective-permute-done = bf16[384,1024]{1,0:T(8,128)(2,1)S(1)} collective-permute-done((bf16[384,1024]{1,0:T(8,128)(2,1)S(1)}, bf16[384,1024]{1,0:T(8,128)(2,1)S(1)}, u32[]{:S(2)}, u32[]{:S(2)}) %collective-permute-start) | collective-permute-done | bytes 786464 | tf_op jit(solution)/shard_map/ppermute | solution.py:93
  335.1 7.5 %collective-permute-done.7 = bf16[384,1024]{1,0:T(8,128)(2,1)S(1)} collective-permute-done((bf16[384,1024]{1,0:T(8,128)(2,1)S(1)}, bf16[384,1024]{1,0:T(8,128)(2,1)S(1)}, u32[]{:S(2)}, u32[]{:S(2)}) %collective-permute-start.7) | collective-permute-done | bytes 786464 | tf_op jit(solution)/shard_map/ppermute | solution.py:93
  343.7 8.8 %collective-permute-done.1 = bf16[384,1024]{1,0:T(8,128)(2,1)S(1)} collective-permute-done((bf16[384,1024]{1,0:T(8,128)(2,1)S(1)}, bf16[384,1024]{1,0:T(8,128)(2,1)S(1)}, u32[]{:S(2)}, u32[]{:S(2)}) %collective-permute-start.1) | collective-permute-done | bytes 786464 | tf_op jit(solution)/shard_map/ppermute | solution.py:93
  353.7 7.1 %collective-permute-done.8 = bf16[384,1024]{1,0:T(8,128)(2,1)S(1)} collective-permute-done((bf16[384,1024]{1,0:T(8,128)(2,1)S(1)}, bf16[384,1024]{1,0:T(8,128)(2,1)S(1)}, u32[]{:S(2)}, u32[]{:S(2)}) %collective-permute-start.8) | collective-permute-done | bytes 786464 | tf_op jit(solution)/shard_map/ppermute | solution.py:93
  362.3 8.3 %collective-permute-done.2 = bf16[384,1024]{1,0:T(8,128)(2,1)S(1)} collective-permute-done((bf16[384,1024]{1,0:T(8,128)(2,1)S(1)}, bf16[384,1024]{1,0:T(8,128)(2,1)S(1)}, u32[]{:S(2)}, u32[]{:S(2)}) %collective-permute-start.2) | collective-permute-done | bytes 786464 | tf_op jit(solution)/shard_map/ppermute | solution.py:93
  371.3 7.2 %collective-permute-done.9 = bf16[384,1024]{1,0:T(8,128)(2,1)S(1)} collective-permute-done((bf16[384,1024]{1,0:T(8,128)(2,1)S(1)}, bf16[384,1024]{1,0:T(8,128)(2,1)S(1)}, u32[]{:S(2)}, u32[]{:S(2)}) %collective-permute-start.9) | collective-permute-done | bytes 786464 | tf_op jit(solution)/shard_map/ppermute | solution.py:93
  380.0 7.6 %collective-permute-done.3 = bf16[384,1024]{1,0:T(8,128)(2,1)S(1)} collective-permute-done((bf16[384,1024]{1,0:T(8,128)(2,1)S(1)}, bf16[384,1024]{1,0:T(8,128)(2,1)S(1)}, u32[]{:S(2)}, u32[]{:S(2)}) %collective-permute-start.3) | collective-permute-done | bytes 786464 | tf_op jit(solution)/shard_map/ppermute | solution.py:93
  389.0 6.1 collective-permute-done.10
  406.9 21.1 %collective-permute-done.11 = bf16[384,1024]{1,0:T(8,128)(2,1)} collective-permute-done((bf16[384,1024]{1,0:T(8,128)(2,1)}, bf16[384,1024]{1,0:T(8,128)(2,1)}, u32[]{:S(2)}, u32[]{:S(2)}) %collective-permute-start.11) | collective-permute-done | bytes 786464 | tf_op jit(solution)/shard_map/ppermute | solution.py:93
  430.3 8.6 %collective-permute-done.5 = bf16[384,1024]{1,0:T(8,128)(2,1)S(1)} collective-permute-done((bf16[384,1024]{1,0:T(8,128)(2,1)S(1)}, bf16[384,1024]{1,0:T(8,128)(2,1)S(1)}, u32[]{:S(2)}, u32[]{:S(2)}) %collective-permute-start.5) | collective-permute-done | bytes 786464 | tf_op jit(solution)/shard_map/ppermute | solution.py:93
  440.1 9.1 %collective-permute-start.6 = (bf16[384,1024]{1,0:T(8,128)(2,1)}, bf16[384,1024]{1,0:T(8,128)(2,1)}, u32[]{:S(2)}, u32[]{:S(2)}) collective-permute-start(bf16[384,1024]{1,0:T(8,128)(2,1)} %add_convert_fusion.10), channel_id=1, source_target_pairs={{0,1},{1,2},{2,3},{3,7},{7,6},{6,5},{5,4},{4,0},{8,9},{9,10},{10,1... | collective-permute-start | bytes 2359304 | tf_op jit(solution)/shard_map/ppermute | solution.py:93
  449.2 80.1 %all-reduce.3.cloned.1.call-done = bf16[272,3072]{0,1:T(8,128)(2,1)} async-done(((bf16[272,3072]{0,1:T(8,128)(2,1)}), bf16[272,3072]{0,1:T(8,128)(2,1)}) %all-reduce.3.cloned.1.call-update) | async-done | bytes 1671184 | tf_op jit(solution)/shard_map/psum | solution.py:303
  539.5 14.8 %collective-permute-done.13 = bf16[384,1024]{1,0:T(8,128)(2,1)} collective-permute-done((bf16[384,1024]{1,0:T(8,128)(2,1)}, bf16[384,1024]{1,0:T(8,128)(2,1)}, u32[]{:S(2)}, u32[]{:S(2)}) %collective-permute-start.13) | collective-permute-done | bytes 786464 | tf_op jit(solution)/shard_map/ppermute | solution.py:93
  581.2 11.8 %collective-permute-done.16 = bf16[384,1024]{1,0:T(8,128)(2,1)S(1)} collective-permute-done((bf16[384,1024]{1,0:T(8,128)(2,1)S(1)}, bf16[384,1024]{1,0:T(8,128)(2,1)S(1)}, u32[]{:S(2)}, u32[]{:S(2)}) %collective-permute-start.16) | collective-permute-done | bytes 786464 | tf_op jit(solution)/shard_map/ppermute | solution.py:102
  598.9 11.6 %collective-permute-done.18 = bf16[384,1024]{1,0:T(8,128)(2,1)S(1)} collective-permute-done((bf16[384,1024]{1,0:T(8,128)(2,1)S(1)}, bf16[384,1024]{1,0:T(8,128)(2,1)S(1)}, u32[]{:S(2)}, u32[]{:S(2)}) %collective-permute-start.18) | collective-permute-done | bytes 786464 | tf_op jit(solution)/shard_map/ppermute | solution.py:102
  616.5 11.6 %collective-permute-done.20 = bf16[384,1024]{1,0:T(8,128)(2,1)} collective-permute-done((bf16[384,1024]{1,0:T(8,128)(2,1)S(1)}, bf16[384,1024]{1,0:T(8,128)(2,1)}, u32[]{:S(2)}, u32[]{:S(2)}) %collective-permute-start.20) | collective-permute-done | bytes 786464 | tf_op jit(solution)/shard_map/ppermute | solution.py:102
  639.0 6.8 collective-permute-done.22
  655.6 7.8 %collective-permute-done.24 = bf16[384,1024]{1,0:T(8,128)(2,1)} collective-permute-done((bf16[384,1024]{1,0:T(8,128)(2,1)}, bf16[384,1024]{1,0:T(8,128)(2,1)}, u32[]{:S(2)}, u32[]{:S(2)}) %collective-permute-start.24) | collective-permute-done | bytes 786464 | tf_op jit(solution)/shard_map/ppermute | solution.py:102
  687.0 6.8 slice_convert_fusion
  (387 shorter events, 287.2 us)
Async XLA Ops:
  7.2 33.5 %all-gather.7.cloned.1.call-start = ((), (), s32[]{:S(2)}) async-start(), calls=%async_computation.4 | async-start | bytes 1572864 | tf_op jit(solution)/shard_map/all_gather | solution.py:149
  16.5 49.8 %all-gather.13.cloned.1.call-start = ((), (), s32[]{:S(2)}) async-start(), calls=%async_computation.11 | async-start | bytes 2621440 | tf_op jit(solution)/shard_map/all_gather | solution.py:133
  17.3 72.6 %all-gather.9.cloned.1.call-start = ((), (), s32[]{:S(2)}) async-start(), calls=%async_computation.5 | async-start | bytes 2621440 | tf_op jit(solution)/shard_map/all_gather | solution.py:176
  59.9 118.7 %reduce-scatter.7.cloned.1.call-start = ((), (), s32[]{:S(2)}) async-start(), calls=%async_computation.6 | async-start | bytes 2949120 | tf_op jit(solution)/shard_map/reduce_scatter | solution.py:227
  145.3 67.8 %reduce-scatter.9.cloned.1.call-start = ((), (), s32[]{:S(2)}) async-start(), calls=%async_computation.7 | async-start | bytes 2621440 | tf_op jit(solution)/shard_map/reduce_scatter | solution.py:229
  180.7 76.9 %reduce-scatter.11.cloned.1.call-start = ((), (), s32[]{:S(2)}) async-start(), calls=%async_computation.8 | async-start | bytes 1572864 | tf_op jit(solution)/shard_map/reduce_scatter | solution.py:260
  237.2 160.4 %reduce-scatter.13.cloned.1.call-start = ((), (), s32[]{:S(2)}) async-start(), calls=%async_computation.12 | async-start | bytes 8355840
  280.9 248.5 %all-reduce.3.cloned.1.call-start = ((), (), s32[]{:S(2)}) async-start(), calls=%async_computation.9 | async-start | bytes 4718592 | tf_op jit(solution)/shard_map/psum | solution.py:303
  313.9 19.6 %collective-permute-start = (bf16[384,1024]{1,0:T(8,128)(2,1)S(1)}, bf16[384,1024]{1,0:T(8,128)(2,1)S(1)}, u32[]{:S(2)}, u32[]{:S(2)}) collective-permute-start(bf16[384,1024]{1,0:T(8,128)(2,1)S(1)} %pad_maximum_fusion.7), channel_id=1, source_target_pairs={{0,1},{1,2},{2,3},{3,7},{7,6},{6,5},{5,4},{4,0},{8,9},{9,10},{10,1... | collective-permute-start | bytes 2359304 | tf_op jit(solution)/shard_map/ppermute | solution.py:93
  323.8 18.8 %collective-permute-start.7 = (bf16[384,1024]{1,0:T(8,128)(2,1)S(1)}, bf16[384,1024]{1,0:T(8,128)(2,1)S(1)}, u32[]{:S(2)}, u32[]{:S(2)}) collective-permute-start(bf16[384,1024]{1,0:T(8,128)(2,1)S(1)} %pad_maximum_fusion.8), channel_id=1, source_target_pairs={{0,4},{1,0},{2,1},{3,2},{7,3},{6,7},{5,6},{4,5},{8,12},{9,8},{10,9... | collective-permute-start | bytes 2359304 | tf_op jit(solution)/shard_map/ppermute | solution.py:93
  333.8 18.7 %collective-permute-start.1 = (bf16[384,1024]{1,0:T(8,128)(2,1)S(1)}, bf16[384,1024]{1,0:T(8,128)(2,1)S(1)}, u32[]{:S(2)}, u32[]{:S(2)}) collective-permute-start(bf16[384,1024]{1,0:T(8,128)(2,1)S(1)} %add_convert_fusion.15), channel_id=1, source_target_pairs={{0,1},{1,2},{2,3},{3,7},{7,6},{6,5},{5,4},{4,0},{8,9},{9,10},{10,1... | collective-permute-start | bytes 2359304 | tf_op jit(solution)/shard_map/ppermute | solution.py:93
  342.9 17.9 %collective-permute-start.8 = (bf16[384,1024]{1,0:T(8,128)(2,1)S(1)}, bf16[384,1024]{1,0:T(8,128)(2,1)S(1)}, u32[]{:S(2)}, u32[]{:S(2)}) collective-permute-start(bf16[384,1024]{1,0:T(8,128)(2,1)S(1)} %add_convert_fusion.8), channel_id=1, source_target_pairs={{0,4},{1,0},{2,1},{3,2},{7,3},{6,7},{5,6},{4,5},{8,12},{9,8},{10,9... | collective-permute-start | bytes 2359304 | tf_op jit(solution)/shard_map/ppermute | solution.py:93
  352.8 17.7 %collective-permute-start.2 = (bf16[384,1024]{1,0:T(8,128)(2,1)S(1)}, bf16[384,1024]{1,0:T(8,128)(2,1)S(1)}, u32[]{:S(2)}, u32[]{:S(2)}) collective-permute-start(bf16[384,1024]{1,0:T(8,128)(2,1)S(1)} %add_convert_fusion.14), channel_id=1, source_target_pairs={{0,1},{1,2},{2,3},{3,7},{7,6},{6,5},{5,4},{4,0},{8,9},{9,10},{10,1... | collective-permute-start | bytes 2359304 | tf_op jit(solution)/shard_map/ppermute | solution.py:93
  361.1 17.4 %collective-permute-start.9 = (bf16[384,1024]{1,0:T(8,128)(2,1)S(1)}, bf16[384,1024]{1,0:T(8,128)(2,1)S(1)}, u32[]{:S(2)}, u32[]{:S(2)}) collective-permute-start(bf16[384,1024]{1,0:T(8,128)(2,1)S(1)} %add_convert_fusion.7), channel_id=1, source_target_pairs={{0,4},{1,0},{2,1},{3,2},{7,3},{6,7},{5,6},{4,5},{8,12},{9,8},{10,9... | collective-permute-start | bytes 2359304 | tf_op jit(solution)/shard_map/ppermute | solution.py:93
  396.3 31.7 %collective-permute-start.11 = (bf16[384,1024]{1,0:T(8,128)(2,1)}, bf16[384,1024]{1,0:T(8,128)(2,1)}, u32[]{:S(2)}, u32[]{:S(2)}) collective-permute-start(bf16[384,1024]{1,0:T(8,128)(2,1)} %add_convert_fusion.5), channel_id=1, source_target_pairs={{0,4},{1,0},{2,1},{3,2},{7,3},{6,7},{5,6},{4,5},{8,12},{9,8},{10,9... | collective-permute-start | bytes 2359304 | tf_op jit(solution)/shard_map/ppermute | solution.py:93
  401.5 284.1 %all-gather.11.cloned.1.call-start = ((), (), s32[]{:S(2)}) async-start(), calls=%async_computation.10 | async-start | bytes 8355840 | tf_op jit(solution)/shard_map/all_gather | solution.py:304
  406.7 32.3 %collective-permute-start.5 = (bf16[384,1024]{1,0:T(8,128)(2,1)S(1)}, bf16[384,1024]{1,0:T(8,128)(2,1)S(1)}, u32[]{:S(2)}, u32[]{:S(2)}) collective-permute-start(bf16[384,1024]{1,0:T(8,128)(2,1)S(1)} %add_convert_fusion.11), channel_id=1, source_target_pairs={{0,1},{1,2},{2,3},{3,7},{7,6},{6,5},{5,4},{4,0},{8,9},{9,10},{10,1... | collective-permute-start | bytes 2359304 | tf_op jit(solution)/shard_map/ppermute | solution.py:93
  430.3 103.0 %collective-permute-start.12 = (bf16[384,1024]{1,0:T(8,128)(2,1)}, bf16[384,1024]{1,0:T(8,128)(2,1)}, u32[]{:S(2)}, u32[]{:S(2)}) collective-permute-start(bf16[384,1024]{1,0:T(8,128)(2,1)} %add_convert_fusion.4), channel_id=1, source_target_pairs={{0,4},{1,0},{2,1},{3,2},{7,3},{6,7},{5,6},{4,5},{8,12},{9,8},{10,9... | collective-permute-start | bytes 2359304 | tf_op jit(solution)/shard_map/ppermute | solution.py:93
  440.1 97.2 %collective-permute-start.6 = (bf16[384,1024]{1,0:T(8,128)(2,1)}, bf16[384,1024]{1,0:T(8,128)(2,1)}, u32[]{:S(2)}, u32[]{:S(2)}) collective-permute-start(bf16[384,1024]{1,0:T(8,128)(2,1)} %add_convert_fusion.10), channel_id=1, source_target_pairs={{0,1},{1,2},{2,3},{3,7},{7,6},{6,5},{5,4},{4,0},{8,9},{9,10},{10,1... | collective-permute-start | bytes 2359304 | tf_op jit(solution)/shard_map/ppermute | solution.py:93
  535.8 18.5 %collective-permute-start.13 = (bf16[384,1024]{1,0:T(8,128)(2,1)}, bf16[384,1024]{1,0:T(8,128)(2,1)}, u32[]{:S(2)}, u32[]{:S(2)}) collective-permute-start(bf16[384,1024]{1,0:T(8,128)(2,1)} %add_convert_fusion.3), channel_id=1, source_target_pairs={{0,4},{1,0},{2,1},{3,2},{7,3},{6,7},{5,6},{4,5},{8,12},{9,8},{10,9... | collective-permute-start | bytes 2359304 | tf_op jit(solution)/shard_map/ppermute | solution.py:93
  539.0 36.3 %collective-permute-start.14 = (bf16[384,1024]{1,0:T(8,128)(2,1)S(1)}, bf16[384,1024]{1,0:T(8,128)(2,1)S(1)}, u32[]{:S(2)}, u32[]{:S(2)}) collective-permute-start(bf16[384,1024]{1,0:T(8,128)(2,1)S(1)} %add_convert_fusion.9), channel_id=1, source_target_pairs={{0,1},{1,2},{2,3},{3,7},{7,6},{6,5},{5,4},{4,0},{8,9},{9,10},{10,1... | collective-permute-start | bytes 2359304 | tf_op jit(solution)/shard_map/ppermute | solution.py:102
  555.7 20.2 %collective-permute-start.15 = (bf16[384,1024]{1,0:T(8,128)(2,1)S(1)}, bf16[384,1024]{1,0:T(8,128)(2,1)S(1)}, u32[]{:S(2)}, u32[]{:S(2)}) collective-permute-start(bf16[384,1024]{1,0:T(8,128)(2,1)S(1)} %add_convert_fusion.2), channel_id=1, source_target_pairs={{0,4},{1,0},{2,1},{3,2},{7,3},{6,7},{5,6},{4,5},{8,12},{9,8},{10,9... | collective-permute-start | bytes 2359304 | tf_op jit(solution)/shard_map/ppermute | solution.py:102
  575.3 17.7 %collective-permute-start.16 = (bf16[384,1024]{1,0:T(8,128)(2,1)S(1)}, bf16[384,1024]{1,0:T(8,128)(2,1)S(1)}, u32[]{:S(2)}, u32[]{:S(2)}) collective-permute-start(bf16[384,1024]{1,0:T(8,128)(2,1)S(1)} %collective-permute-done.14), channel_id=1, source_target_pairs={{0,1},{1,2},{2,3},{3,7},{7,6},{6,5},{5,4},{4,0},{8,9},{9,10},{10,1... | collective-permute-start | bytes 2359304 | tf_op jit(solution)/shard_map/ppermute | solution.py:102
  575.9 17.7 %collective-permute-start.17 = (bf16[384,1024]{1,0:T(8,128)(2,1)S(1)}, bf16[384,1024]{1,0:T(8,128)(2,1)S(1)}, u32[]{:S(2)}, u32[]{:S(2)}) collective-permute-start(bf16[384,1024]{1,0:T(8,128)(2,1)S(1)} %collective-permute-done.15), channel_id=1, source_target_pairs={{0,4},{1,0},{2,1},{3,2},{7,3},{6,7},{5,6},{4,5},{8,12},{9,8},{10,9... | collective-permute-start | bytes 2359304 | tf_op jit(solution)/shard_map/ppermute | solution.py:102
  593.0 17.5 %collective-permute-start.18 = (bf16[384,1024]{1,0:T(8,128)(2,1)S(1)}, bf16[384,1024]{1,0:T(8,128)(2,1)S(1)}, u32[]{:S(2)}, u32[]{:S(2)}) collective-permute-start(bf16[384,1024]{1,0:T(8,128)(2,1)S(1)} %collective-permute-done.16), channel_id=1, source_target_pairs={{0,1},{1,2},{2,3},{3,7},{7,6},{6,5},{5,4},{4,0},{8,9},{9,10},{10,1... | collective-permute-start | bytes 2359304 | tf_op jit(solution)/shard_map/ppermute | solution.py:102
  593.6 17.5 %collective-permute-start.19 = (bf16[384,1024]{1,0:T(8,128)(2,1)S(1)}, bf16[384,1024]{1,0:T(8,128)(2,1)S(1)}, u32[]{:S(2)}, u32[]{:S(2)}) collective-permute-start(bf16[384,1024]{1,0:T(8,128)(2,1)S(1)} %collective-permute-done.17), channel_id=1, source_target_pairs={{0,4},{1,0},{2,1},{3,2},{7,3},{6,7},{5,6},{4,5},{8,12},{9,8},{10,9... | collective-permute-start | bytes 2359304 | tf_op jit(solution)/shard_map/ppermute | solution.py:102
  610.6 17.5 %collective-permute-start.20 = (bf16[384,1024]{1,0:T(8,128)(2,1)S(1)}, bf16[384,1024]{1,0:T(8,128)(2,1)}, u32[]{:S(2)}, u32[]{:S(2)}) collective-permute-start(bf16[384,1024]{1,0:T(8,128)(2,1)S(1)} %collective-permute-done.18), channel_id=1, source_target_pairs={{0,1},{1,2},{2,3},{3,7},{7,6},{6,5},{5,4},{4,0},{8,9},{9,10},{10,1... | collective-permute-start | bytes 2359304 | tf_op jit(solution)/shard_map/ppermute | solution.py:102
  611.1 17.5 %collective-permute-start.21 = (bf16[384,1024]{1,0:T(8,128)(2,1)S(1)}, bf16[384,1024]{1,0:T(8,128)(2,1)}, u32[]{:S(2)}, u32[]{:S(2)}) collective-permute-start(bf16[384,1024]{1,0:T(8,128)(2,1)S(1)} %collective-permute-done.19), channel_id=1, source_target_pairs={{0,4},{1,0},{2,1},{3,2},{7,3},{6,7},{5,6},{4,5},{8,12},{9,8},{10,9... | collective-permute-start | bytes 2359304 | tf_op jit(solution)/shard_map/ppermute | solution.py:102
  628.1 17.7 %collective-permute-start.22 = (bf16[384,1024]{1,0:T(8,128)(2,1)}, bf16[384,1024]{1,0:T(8,128)(2,1)}, u32[]{:S(2)}, u32[]{:S(2)}) collective-permute-start(bf16[384,1024]{1,0:T(8,128)(2,1)} %collective-permute-done.20), channel_id=1, source_target_pairs={{0,1},{1,2},{2,3},{3,7},{7,6},{6,5},{5,4},{4,0},{8,9},{9,10},{10,1... | collective-permute-start | bytes 2359304 | tf_op jit(solution)/shard_map/ppermute | solution.py:102
  628.6 17.7 %collective-permute-start.23 = (bf16[384,1024]{1,0:T(8,128)(2,1)}, bf16[384,1024]{1,0:T(8,128)(2,1)}, u32[]{:S(2)}, u32[]{:S(2)}) collective-permute-start(bf16[384,1024]{1,0:T(8,128)(2,1)} %collective-permute-done.21), channel_id=1, source_target_pairs={{0,4},{1,0},{2,1},{3,2},{7,3},{6,7},{5,6},{4,5},{8,12},{9,8},{10,9... | collective-permute-start | bytes 2359304 | tf_op jit(solution)/shard_map/ppermute | solution.py:102
  645.8 17.7 %collective-permute-start.24 = (bf16[384,1024]{1,0:T(8,128)(2,1)}, bf16[384,1024]{1,0:T(8,128)(2,1)}, u32[]{:S(2)}, u32[]{:S(2)}) collective-permute-start(bf16[384,1024]{1,0:T(8,128)(2,1)} %collective-permute-done.22), channel_id=1, source_target_pairs={{0,1},{1,2},{2,3},{3,7},{7,6},{6,5},{5,4},{4,0},{8,9},{9,10},{10,1... | collective-permute-start | bytes 2359304 | tf_op jit(solution)/shard_map/ppermute | solution.py:102
  646.3 17.7 %collective-permute-start.25 = (bf16[384,1024]{1,0:T(8,128)(2,1)}, bf16[384,1024]{1,0:T(8,128)(2,1)}, u32[]{:S(2)}, u32[]{:S(2)}) collective-permute-start(bf16[384,1024]{1,0:T(8,128)(2,1)} %collective-permute-done.23), channel_id=1, source_target_pairs={{0,4},{1,0},{2,1},{3,2},{7,3},{6,7},{5,6},{4,5},{8,12},{9,8},{10,9... | collective-permute-start | bytes 2359304 | tf_op jit(solution)/shard_map/ppermute | solution.py:102
  (80 other events, 672.7 us)
Sparse Core Ops, SparseCore 0:
  16.6 24.0 all-gather.6
  42.3 22.5 all-gather.12
  67.0 22.8 all-gather.8
  145.4 33.0 reduce-scatter.6
  181.6 31.4 reduce-scatter.8
  237.3 20.3 reduce-scatter.10
  281.0 60.9 reduce-scatter.12
  401.6 127.7 all-reduce.2
  533.5 47.6 all-gather.10
